TPU v7x, 32 devices: a whole 2x2x4 slice. The times are simulated.
32 devices in a mesh: groups: 2 (over y), docs: 4 (over z), proj: 4 (over x, core).
Axes of the slice: x: 2, y: 2, z: 4, core: 2. Of those that a mesh axis runs over, the one named last changes fastest.
Arguments:
- queries: bfloat16 [1216, 65536], P(('groups', 'docs'), 'proj'), parts along dimension 0, may hold values from -6 to 6
- store: bfloat16 [1280, 65536], P(('groups', 'docs'), 'proj'), parts along dimension 0, may hold values from -0.0234375 to 0.0234375
Outputs:
- scores: float32 [608, 1280], P('proj', ('groups', 'docs')), parts along dimension 1
There are 2 independent parts, one for each index of `groups`. A program takes and returns all parts, laid end to end along the dimension named above; each array names one. Nothing has to cross between parts.
All inputs are finite; a program needn't handle non-finite values.
Results may differ from a plain program's by a relative error of at most 0.0003.
Values may be sent and summed in bfloat16 or wider, within the bound.
No kernel may reach another device: no remote copies, remote signals or barrier semaphores. Data moves between devices by JAX's collectives and lax.ppermute only.
A program may use at most 64 MiB of HBM per device.

v0:
```python
import jax
import jax.numpy as jnp
from jax import lax
from jax.sharding import PartitionSpec as P


def from_behind(value, axis, steps):
    count = lax.axis_size(axis)
    pairs = [(source, (source + steps) % count) for source in range(count)]
    return lax.ppermute(value, axis, pairs)


def per_device(queries, store):
    one_ahead = from_behind(queries, "docs", -1)
    two_ahead = from_behind(one_ahead, "docs", -1)
    three_ahead = from_behind(two_ahead, "docs", -1)
    stacked = jnp.concatenate([queries, one_ahead, two_ahead, three_ahead], axis=0)
    return lax.psum_scatter(
        lax.dot_general(
            stacked, store, (((1,), (1,)), ((), ())), preferred_element_type=jnp.float32
        ),
        "proj",
        scatter_dimension=0,
        tiled=True,
    )


def solution(mesh):
    placed = (P(("groups", "docs"), "proj"), P(("groups", "docs"), "proj"))
    return jax.shard_map(
        per_device,
        mesh=mesh,
        in_specs=placed,
        out_specs=P("proj", ("groups", "docs")),
        check_vma=False,
    )
```

profile of v0, /device:TPU:18, one launch (start us, length us, event | category | flops | bytes accessed | tf_op | source)
XLA Modules:
  0.0 379.1 jit_solution(10550142904528258670)
XLA Ops:
  6.5 0.0 reduce-scatter.2.cloned.1.call-start
  6.5 0.4 collective-permute-start
  7.0 108.9 %collective-permute-done = bf16[152,16384]{1,0:T(8,128)(2,1)S(1)} collective-permute-done((bf16[152,16384]{1,0:T(8,128)(2,1)}, bf16[152,16384]{1,0:T(8,128)(2,1)S(1)}, u32[]{:S(2)}, u32[]{:S(2)}) %collective-permute-start) | collective-permute-done | bytes 4980768 | tf_op jit(solution)/shard_map/ppermute | solution.py:10
  115.9 0.4 collective-permute-start.1
  116.4 109.5 %collective-permute-done.1 = bf16[152,16384]{1,0:T(8,128)(2,1)S(1)} collective-permute-done((bf16[152,16384]{1,0:T(8,128)(2,1)S(1)}, bf16[152,16384]{1,0:T(8,128)(2,1)S(1)}, u32[]{:S(2)}, u32[]{:S(2)}) %collective-permute-start.1) | collective-permute-done | bytes 4980768 | tf_op jit(solution)/shard_map/ppermute | solution.py:10
  225.8 0.0 copy-start
  225.8 2.3 copy-done
  228.1 0.0 collective-permute-start.2
  228.1 109.3 %collective-permute-done.2 = bf16[152,16384]{1,0:T(8,128)(2,1)} collective-permute-done((bf16[152,16384]{1,0:T(8,128)(2,1)S(1)}, bf16[152,16384]{1,0:T(8,128)(2,1)}, u32[]{:S(2)}, u32[]{:S(2)}) %collective-permute-start.2) | collective-permute-done | bytes 4980768 | tf_op jit(solution)/shard_map/ppermute | solution.py:10
  337.4 10.4 %fusion = f32[608,160]{1,0:T(8,128)} fusion(bf16[160,16384]{1,0:T(8,128)(2,1)} %param.3, bf16[152,16384]{1,0:T(8,128)(2,1)} %collective-permute-done.2, bf16[152,16384]{1,0:T(8,128)(2,1)} %copy-done, bf16[152,16384]{1,0:T(8,128)(2,1)S(1)} %collective-permute-done, bf16[152,16384]{1,0:T(8,128)(2,1)} %param.2), kind=kOutput, calls=%fused_computation | convolution fusion | flops 3267362816 | bytes 25554944 | tf_op jit(solution)/shard_map/dot_general | solution.py:19
  347.7 0.0 reduce-scatter.2.cloned.1.call-update
  347.8 24.5 %reduce-scatter.2.cloned.1.call-done = f32[152,160]{1,0:T(8,128)} async-done(((f32[608,160]{1,0:T(8,128)}), f32[152,160]{1,0:T(8,128)}) %reduce-scatter.2.cloned.1.call-update) | async-done | bytes 97296 | tf_op jit(solution)/shard_map/reduce_scatter | solution.py:18
Async XLA Ops:
  6.5 365.7 %reduce-scatter.2.cloned.1.call-start = ((), (), s32[]{:S(2)}) async-start(), calls=%async_computation.1 | async-start | bytes 778240 | tf_op jit(solution)/shard_map/reduce_scatter | solution.py:18
  6.5 109.4 %collective-permute-start = (bf16[152,16384]{1,0:T(8,128)(2,1)}, bf16[152,16384]{1,0:T(8,128)(2,1)S(1)}, u32[]{:S(2)}, u32[]{:S(2)}) collective-permute-start(bf16[152,16384]{1,0:T(8,128)(2,1)} %param.2), channel_id=1, source_target_pairs={{0,12},{4,0},{8,4},{12,8},{1,13},{5,1},{9,5},{13,9},{2,14},{6,2},{... | collective-permute-start | bytes 14942216 | tf_op jit(solution)/shard_map/ppermute | solution.py:10
  115.9 109.9 %collective-permute-start.1 = (bf16[152,16384]{1,0:T(8,128)(2,1)S(1)}, bf16[152,16384]{1,0:T(8,128)(2,1)S(1)}, u32[]{:S(2)}, u32[]{:S(2)}) collective-permute-start(bf16[152,16384]{1,0:T(8,128)(2,1)S(1)} %collective-permute-done), channel_id=1, source_target_pairs={{0,12},{4,0},{8,4},{12,8},{1,13},{5,1},{9,5},{13,9},{2,14},{6,2},{... | collective-permute-start | bytes 14942216 | tf_op jit(solution)/shard_map/ppermute | solution.py:10
  225.8 2.3 copy-start
  228.1 109.3 %collective-permute-start.2 = (bf16[152,16384]{1,0:T(8,128)(2,1)S(1)}, bf16[152,16384]{1,0:T(8,128)(2,1)}, u32[]{:S(2)}, u32[]{:S(2)}) collective-permute-start(bf16[152,16384]{1,0:T(8,128)(2,1)S(1)} %collective-permute-done.1), channel_id=1, source_target_pairs={{0,12},{4,0},{8,4},{12,8},{1,13},{5,1},{9,5},{13,9},{2,14},{6,2},{... | collective-permute-start | bytes 14942216 | tf_op jit(solution)/shard_map/ppermute | solution.py:10
Sparse Core Ops, SparseCore 0:
  347.9 24.3 reduce-scatter.1
where the time goes:
time: 382 us; the launch traced here: 379 us
  waiting for transfers between devices  352 us (92%)
  between operations  13.4 us (4%)
  matrix products  10.4 us (3%)
    ppermute x3, waiting for transfers between devices, from_behind(): return lax.ppermute(value, axis, pairs)  328 us
    reduce_scatter x1, waiting for transfers between devices, per_device(): lax.psum_scatter(lax.dot_general(stacked, store, (((1,), (1,)), ((), ()))...  24.5 us
    dot_general x1, matrix products, per_device(): lax.dot_general(stacked, store, (((1,), (1,)), ((), ())), preferred_eleme...  10.4 us
  transfers between devices with their start and end apart: 4, of which 4 were waited for; matrix products, arithmetic and copies ran while one was open for 0% of the time, Pallas kernels for 0%

commit v1 on v0

v1 whole, which is shorter than its diff:
```python
import jax
import jax.numpy as jnp
from jax import lax
from jax.sharding import PartitionSpec as P

WINDOW = 4
LINE = 4


def from_behind(value, axis, steps):
    count = lax.axis_size(axis)
    pairs = [(source, (source + steps) % count) for source in range(count)]
    return lax.ppermute(value, axis, pairs)


def products(rows, docs):
    return lax.dot_general(
        rows, docs, (((1,), (1,)), ((), ())), preferred_element_type=jnp.float32
    )


def ring(queries, store):
    blocks = [queries]
    for _ in range(WINDOW - 1):
        blocks.append(from_behind(blocks[-1], "docs", -1))
    return lax.psum_scatter(
        products(jnp.concatenate(blocks, axis=0), store),
        "proj",
        scatter_dimension=0,
        tiled=True,
    )


def after(value, *others):
    return lax.optimization_barrier((value,) + others)[0]


ENDS = [(0, 1), (1, 0), (2, 3), (3, 2)]
MIDDLE = [(1, 2), (2, 1)]
OUTWARD = [(1, 0), (2, 3)]
INWARD = [(0, 1), (3, 2)]
CORES = [(0, 1), (1, 0), (2, 3), (3, 2)]
CHIPS = [(0, 2), (1, 3), (2, 0), (3, 1)]


def along(value, pairs):
    return lax.ppermute(value, "docs", pairs)


def line(queries, store):
    depth = queries.shape[1]
    cut = depth // 4 // 128 * 128
    last = depth * 7 // 8 // 128 * 128
    place = lax.axis_index("docs")
    share = lax.axis_index("proj")
    inner = (place == 1) | (place == 2)
    left = place < 2
    near_store, far_store = store[:, :cut], store[:, cut:]

    middle = along(queries, MIDDLE)
    ends_near = along(queries[:, :cut], ENDS)
    ends_rest = along(after(queries[:, cut:], ends_near), ENDS)
    far_near = along(ends_near, MIDDLE)
    ends_held = after(ends_rest, middle)
    far_body = along(ends_held[:, : last - cut], MIDDLE)
    relayed = along(middle[:, :cut], OUTWARD)
    outer_store = along(after(far_store, ends_rest), INWARD)
    far_relayed = along(after(far_near, relayed), OUTWARD)
    far_tail = along(after(ends_rest[:, last - cut :], far_relayed), MIDDLE)

    own_part = products(queries, store)
    ends_part = products(ends_near, near_store) + products(ends_rest, far_store)
    middle_part = products(middle, store) + products(relayed, near_store)
    far_part = (
        products(far_near, near_store)
        + products(far_relayed, near_store)
        + products(far_body, store[:, cut:last])
        + products(far_tail, store[:, last:])
    )
    help_middle = products(middle[:, cut:], outer_store)
    help_far = products(far_body, outer_store[:, : last - cut]) + products(far_tail, outer_store[:, last - cut :])

    first = own_part
    second = jnp.where(inner & left, middle_part, jnp.where(inner, ends_part, jnp.where(left, ends_part, far_part)))
    third = jnp.where(inner, far_part, middle_part)
    fourth = jnp.where(inner, jnp.where(left, ends_part, middle_part), jnp.where(left, far_part, ends_part))
    return first, second, third, fourth, help_middle, help_far, inner, left, share


def finish(first, second, third, fourth, help_middle, help_far, inner, left, share):
    even = share % 2 == 0
    low = share < 2
    rows = first.shape[0]
    kept = jnp.concatenate([jnp.where(even, first, second), jnp.where(even, third, fourth), jnp.where(even, help_middle, help_far)], axis=0)
    given = jnp.concatenate([jnp.where(even, second, first), jnp.where(even, fourth, third), jnp.where(even, help_far, help_middle)], axis=0)
    total = kept + lax.ppermute(given, "proj", CORES)
    below, above, helped = total[:rows], total[rows : 2 * rows], total[2 * rows :]
    def at(docs, proj):
        return docs * 4 + proj

    one = [
        (at(1, 0), at(0, 2)), (at(1, 1), at(0, 3)),
        (at(2, 0), at(3, 2)), (at(2, 1), at(3, 1)),
    ]
    two = [
        (at(1, 2), at(0, 2)), (at(1, 3), at(0, 3)),
        (at(2, 2), at(3, 2)), (at(2, 3), at(3, 1)),
    ]
    over = lax.ppermute(jnp.where(low, above, below), "proj", CHIPS)
    help_one = lax.ppermute(helped, ("docs", "proj"), one)
    help_two = lax.ppermute(helped, ("docs", "proj"), two)
    return jnp.where(low, below, above) + over + help_one + help_two


def per_device(queries, store):
    if lax.axis_size("docs") == LINE and lax.axis_size("proj") == WINDOW:
        return finish(*line(queries, store))
    return ring(queries, store)


def solution(mesh):
    placed = (P(("groups", "docs"), "proj"), P(("groups", "docs"), "proj"))
    return jax.shard_map(
        per_device,
        mesh=mesh,
        in_specs=placed,
        out_specs=P("proj", ("groups", "docs")),
        check_vma=False,
    )
```

time: 382 us -> 243 us (0.64)
  waiting for transfers between devices: 352 us -> 178 us
  starting transfers between devices: 0.9 us -> 22.2 us
  matrix products: 10.4 us -> 25.5 us
  between operations: 13.4 us -> 0.35 us
  local copies, waits for them, and re-layouts: 2.27 us -> 12.4 us
    ppermute x3 -> x13, waiting for transfers between devices: 328 us -> 178 us  [the longest x9 172 us: along(): return lax.ppermute(value, 'docs', pairs)]
    reduce_scatter x1 -> x0, waiting for transfers between devices: 24.5 us -> none  [per_device(): lax.psum_scatter(lax.dot_general(stacked, store, (((1,), (1,)), ((), ()))...]
    ppermute x3 -> x13, starting transfers between devices: 0.9 us -> 22.2 us  [the longest x9 19.6 us: along(): return lax.ppermute(value, 'docs', pairs)]
    dot_general x1 -> x12, matrix products: 10.4 us -> 25.5 us  [products(): lax.dot_general(rows, docs, (((1,), (1,)), ((), ())), preferred_element_t...]
    slice x0 -> x6, local copies, waits for them, and re-layouts: none -> 9.53 us  [the longest x1 4.39 us: line(): near_store, far_store = (store[:, :cut], store[:, cut:])]
  transfers between devices with their start and end apart: 4 -> 13, of which waited for: 4 -> 8; matrix products, arithmetic and copies ran while one was open for 0% -> 13% of each run, Pallas kernels for 0% -> 0%
where the time goes in v1:
time: 243 us; the launch traced here: 239 us
  waiting for transfers between devices  178 us (73%)
  matrix products  25.5 us (10%)
  starting transfers between devices  22.2 us (9%)
  local copies, waits for them, and re-layouts  12.4 us (5%)
    ppermute x9, waiting for transfers between devices, along(): return lax.ppermute(value, 'docs', pairs)  172 us
    dot_general x12, matrix products, products(): lax.dot_general(rows, docs, (((1,), (1,)), ((), ())), preferred_element_t...  25.5 us
    ppermute x9, starting transfers between devices, along(): return lax.ppermute(value, 'docs', pairs)  19.6 us
  transfers between devices with their start and end apart: 13, of which 8 were waited for; matrix products, arithmetic and copies ran while one was open for 13% of the time, Pallas kernels for 0%

profile of v1, /device:TPU:18, one launch (start us, length us, event | category | flops | bytes accessed | tf_op | source)
XLA Modules:
  0.0 239.0 jit_solution(4917277784669895150)
XLA Ops:
  0.0 2.3 collective-permute-start
  2.4 1.4 slice.47
  3.7 0.3 collective-permute-start.2
  4.0 2.3 slice.48
  6.3 26.4 %collective-permute-done.2 = bf16[152,4096]{1,0:T(8,128)(2,1)} collective-permute-done((bf16[152,4096]{1,0:T(8,128)(2,1)S(1)}, bf16[152,4096]{1,0:T(8,128)(2,1)}, u32[]{:S(2)}, u32[]{:S(2)}) %collective-permute-start.2) | collective-permute-done | bytes 1245216 | tf_op jit(solution)/shard_map/ppermute | solution.py:47
  32.8 0.5 collective-permute-start.3
  33.2 3.3 %collective-permute-start.4 = (bf16[152,4096]{1,0:T(8,128)(2,1)}, bf16[152,4096]{1,0:T(8,128)(2,1)}, u32[]{:S(2)}, u32[]{:S(2)}) collective-permute-start(bf16[152,4096]{1,0:T(8,128)(2,1)} %collective-permute-done.2), channel_id=1, source_target_pairs={{4,8},{8,4},{5,9},{9,5},{6,10},{10,6},{7,11},{11,7},{20,24},{24,20... | collective-permute-start | bytes 3735560 | tf_op jit(solution)/shard_map/ppermute | solution.py:47
  36.5 75.9 %collective-permute-done = bf16[152,16384]{1,0:T(8,128)(2,1)S(1)} collective-permute-done((bf16[152,16384]{1,0:T(8,128)(2,1)}, bf16[152,16384]{1,0:T(8,128)(2,1)S(1)}, u32[]{:S(2)}, u32[]{:S(2)}) %collective-permute-start) | collective-permute-done | bytes 4980768 | tf_op jit(solution)/shard_map/ppermute | solution.py:47
  112.4 1.2 slice.60
  113.6 2.3 collective-permute-start.1
  116.0 1.9 copy-done
  117.8 0.2 slice.50
  118.0 2.4 collective-permute-start.6
  120.4 4.4 %slice.49 = bf16[160,12288]{1,0:T(8,128)(2,1)} slice(bf16[160,16384]{1,0:T(8,128)(2,1)} %param.3), slice={[0:160], [4096:16384]} | slice | bytes 7864320 | tf_op jit(solution)/shard_map/slice | solution.py:58
  124.8 1.5 collective-permute-start.8
  126.4 12.8 %collective-permute-done.4 = bf16[152,4096]{1,0:T(8,128)(2,1)} collective-permute-done((bf16[152,4096]{1,0:T(8,128)(2,1)}, bf16[152,4096]{1,0:T(8,128)(2,1)}, u32[]{:S(2)}, u32[]{:S(2)}) %collective-permute-start.4) | collective-permute-done | bytes 1245216 | tf_op jit(solution)/shard_map/ppermute | solution.py:47
  139.2 0.9 collective-permute-done.1
  140.1 4.5 %collective-permute-start.5 = (bf16[152,4096]{1,0:T(8,128)(2,1)}, bf16[152,4096]{1,0:T(8,128)(2,1)S(1)}, u32[]{:S(2)}, u32[]{:S(2)}) collective-permute-start(bf16[152,4096]{1,0:T(8,128)(2,1)} %collective-permute-done.4), channel_id=1, source_target_pairs={{4,0},{8,12},{5,1},{9,13},{6,2},{10,14},{7,3},{11,15},{20,16},{24,... | collective-permute-start | bytes 3735560 | tf_op jit(solution)/shard_map/ppermute | solution.py:47
  144.5 5.5 %fusion.28 = f32[152,160]{1,0:T(8,128)S(1)} fusion(bf16[152,16384]{1,0:T(8,128)(2,1)} %param.2, bf16[160,16384]{1,0:T(8,128)(2,1)} %param.3), kind=kOutput, calls=%fused_computation.39 | convolution fusion | flops 796917760 | bytes 10320896 | tf_op jit(solution)/shard_map/dot_general | solution.py:17
  150.1 0.0 slice-start
  150.1 0.0 slice-start.2
  150.2 0.0 slice-start.1
  150.2 3.8 %fusion.25 = f32[152,160]{1,0:T(8,128)S(1)} fusion(bf16[152,12288]{1,0:T(8,128)(2,1)S(1)} %copy-done.1, bf16[160,16384]{1,0:T(8,128)(2,1)} %param.3), kind=kOutput, calls=%fused_computation.37 | convolution fusion | flops 597688320 | bytes 7764992 | tf_op jit(solution)/shard_map/dot_general | solution.py:17
  154.0 1.0 slice-done.1
  155.0 1.8 fusion.18
  156.8 11.9 %collective-permute-done.5 = bf16[152,4096]{1,0:T(8,128)(2,1)S(1)} collective-permute-done((bf16[152,4096]{1,0:T(8,128)(2,1)}, bf16[152,4096]{1,0:T(8,128)(2,1)S(1)}, u32[]{:S(2)}, u32[]{:S(2)}) %collective-permute-start.5) | collective-permute-done | bytes 1245216 | tf_op jit(solution)/shard_map/ppermute | solution.py:47
  168.7 2.5 %collective-permute-start.7 = (bf16[152,2048]{1,0:T(8,128)(2,1)S(1)}, bf16[152,2048]{1,0:T(8,128)(2,1)S(1)}, u32[]{:S(2)}, u32[]{:S(2)}) collective-permute-start(bf16[152,2048]{1,0:T(8,128)(2,1)S(1)} %slice.61), channel_id=1, source_target_pairs={{4,8},{8,4},{5,9},{9,5},{6,10},{10,6},{7,11},{11,7},{20,24},{24,20... | collective-permute-start | bytes 1867784 | tf_op jit(solution)/shard_map/ppermute | solution.py:47
  171.3 1.8 convolution_add_fusion.2
  173.1 0.6 fusion.14
  173.6 44.4 %collective-permute-done.7 = bf16[152,2048]{1,0:T(8,128)(2,1)S(1)} collective-permute-done((bf16[152,2048]{1,0:T(8,128)(2,1)S(1)}, bf16[152,2048]{1,0:T(8,128)(2,1)S(1)}, u32[]{:S(2)}, u32[]{:S(2)}) %collective-permute-start.7) | collective-permute-done | bytes 622624 | tf_op jit(solution)/shard_map/ppermute | solution.py:47
  218.0 0.4 fusion.22
  218.4 3.0 %fusion.4 = f32[152,160]{1,0:T(8,128)S(1)} fusion(bf16[152,10240]{1,0:T(8,128)(2,1)} %collective-permute-done.6, bf16[160,16384]{1,0:T(8,128)(2,1)S(1)} %bitcast.17), kind=kOutput, calls=%fused_computation.4 | convolution fusion | flops 498073600 | bytes 6487040 | tf_op jit(solution)/shard_map/dot_general | solution.py:17
  221.4 1.9 fusion.7
  223.2 1.9 broadcast_select_fusion.6
  225.1 0.1 broadcast_select_fusion.2
  225.2 0.4 fusion.20
  225.6 3.1 %fusion.11 = f32[152,160]{1,0:T(8,128)S(1)} fusion(f32[152,160]{1,0:T(8,128)S(1)} %fusion.20, bf16[152,10240]{1,0:T(8,128)(2,1)} %collective-permute-done.6, bf16[160,12288]{1,0:T(8,128)(2,1)S(1)} %collective-permute-done.8), kind=kOutput, calls=%fused_computation.11 | convolution fusion | flops 498097920 | bytes 6642688 | tf_op jit(solution)/shard_map/dot_general | solution.py:17
  228.7 1.4 broadcast_select_fusion.4
  230.2 0.1 collective-permute-start.9
  230.3 1.8 collective-permute-done.9
  232.1 0.1 maximum_add_fusion
  232.2 0.6 collective-permute-start.10
  232.8 1.3 collective-permute-start.12
  234.1 0.7 collective-permute-start.11
  234.7 3.6 %collective-permute-done.10 = f32[152,160]{1,0:T(8,128)S(1)} collective-permute-done((f32[152,160]{1,0:T(8,128)S(1)}, f32[152,160]{1,0:T(8,128)S(1)}, u32[]{:S(2)}, u32[]{:S(2)}) %collective-permute-start.10) | collective-permute-done | bytes 97312 | tf_op jit(solution)/shard_map/ppermute | solution.py:109
  238.3 0.0 collective-permute-done.12
  238.3 0.0 collective-permute-done.11
  238.3 0.7 add_add_fusion
  (17 shorter events, 0.1 us)
Async XLA Ops:
  0.0 112.4 %collective-permute-start = (bf16[152,16384]{1,0:T(8,128)(2,1)}, bf16[152,16384]{1,0:T(8,128)(2,1)S(1)}, u32[]{:S(2)}, u32[]{:S(2)}) collective-permute-start(bf16[152,16384]{1,0:T(8,128)(2,1)} %param.2), channel_id=1, source_target_pairs={{4,8},{8,4},{5,9},{9,5},{6,10},{10,6},{7,11},{11,7},{20,24},{24,20... | collective-permute-start | bytes 14942216 | tf_op jit(solution)/shard_map/ppermute | solution.py:47
  3.7 29.0 %collective-permute-start.2 = (bf16[152,4096]{1,0:T(8,128)(2,1)S(1)}, bf16[152,4096]{1,0:T(8,128)(2,1)}, u32[]{:S(2)}, u32[]{:S(2)}) collective-permute-start(bf16[152,4096]{1,0:T(8,128)(2,1)S(1)} %slice.47), channel_id=1, source_target_pairs={{0,4},{4,0},{8,12},{12,8},{1,5},{5,1},{9,13},{13,9},{2,6},{6,2},{1... | collective-permute-start | bytes 3735560 | tf_op jit(solution)/shard_map/ppermute | solution.py:47
  32.8 83.2 %collective-permute-start.3 = (bf16[152,12288]{1,0:T(8,128)(2,1)S(1)}, bf16[152,12288]{1,0:T(8,128)(2,1)S(1)}, u32[]{:S(2)}, u32[]{:S(2)}) collective-permute-start(bf16[152,12288]{1,0:T(8,128)(2,1)S(1)} %slice.48), channel_id=1, source_target_pairs={{0,4},{4,0},{8,12},{12,8},{1,5},{5,1},{9,13},{13,9},{2,6},{6,2},{1... | collective-permute-start | bytes 11206664 | tf_op jit(solution)/shard_map/ppermute | solution.py:47
  33.2 106.0 %collective-permute-start.4 = (bf16[152,4096]{1,0:T(8,128)(2,1)}, bf16[152,4096]{1,0:T(8,128)(2,1)}, u32[]{:S(2)}, u32[]{:S(2)}) collective-permute-start(bf16[152,4096]{1,0:T(8,128)(2,1)} %collective-permute-done.2), channel_id=1, source_target_pairs={{4,8},{8,4},{5,9},{9,5},{6,10},{10,6},{7,11},{11,7},{20,24},{24,20... | collective-permute-start | bytes 3735560 | tf_op jit(solution)/shard_map/ppermute | solution.py:47
  112.4 8.0 %copy-start.2 = (bf16[152,16384]{1,0:T(8,128)(2,1)}, bf16[152,16384]{1,0:T(8,128)(2,1)S(1)}, u32[]{:S(2)}) copy-start(bf16[152,16384]{1,0:T(8,128)(2,1)S(1)} %collective-permute-done) | copy-start | bytes 14942212
  113.6 26.5 %collective-permute-start.1 = (bf16[152,4096]{1,0:T(8,128)(2,1)}, bf16[152,4096]{1,0:T(8,128)(2,1)}, u32[]{:S(2)}, u32[]{:S(2)}) collective-permute-start(bf16[152,4096]{1,0:T(8,128)(2,1)} %slice.60), channel_id=1, source_target_pairs={{4,0},{8,12},{5,1},{9,13},{6,2},{10,14},{7,3},{11,15},{20,16},{24,... | collective-permute-start | bytes 3735560 | tf_op jit(solution)/shard_map/ppermute | solution.py:47
  116.0 1.9 copy-start
  118.0 100.4 %collective-permute-start.6 = (bf16[152,10240]{1,0:T(8,128)(2,1)S(1)}, bf16[152,10240]{1,0:T(8,128)(2,1)}, u32[]{:S(2)}, u32[]{:S(2)}) collective-permute-start(bf16[152,10240]{1,0:T(8,128)(2,1)S(1)} %slice.50), channel_id=1, source_target_pairs={{4,8},{8,4},{5,9},{9,5},{6,10},{10,6},{7,11},{11,7},{20,24},{24,20... | collective-permute-start | bytes 9338888 | tf_op jit(solution)/shard_map/ppermute | solution.py:47
  124.8 25.3 %copy-start.1 = (bf16[152,12288]{1,0:T(8,128)(2,1)S(1)}, bf16[152,12288]{1,0:T(8,128)(2,1)}, u32[]{:S(2)}) copy-start(bf16[152,12288]{1,0:T(8,128)(2,1)} %copy-done) | copy-start | bytes 11206660
  124.8 100.4 %collective-permute-start.8 = (bf16[160,12288]{1,0:T(8,128)(2,1)}, bf16[160,12288]{1,0:T(8,128)(2,1)S(1)}, u32[]{:S(2)}, u32[]{:S(2)}) collective-permute-start(bf16[160,12288]{1,0:T(8,128)(2,1)} %slice.49), channel_id=1, source_target_pairs={{0,4},{12,8},{1,5},{13,9},{2,6},{14,10},{3,7},{15,11},{16,20},{28,... | collective-permute-start | bytes 11796488 | tf_op jit(solution)/shard_map/ppermute | solution.py:47
  140.1 28.6 %collective-permute-start.5 = (bf16[152,4096]{1,0:T(8,128)(2,1)}, bf16[152,4096]{1,0:T(8,128)(2,1)S(1)}, u32[]{:S(2)}, u32[]{:S(2)}) collective-permute-start(bf16[152,4096]{1,0:T(8,128)(2,1)} %collective-permute-done.4), channel_id=1, source_target_pairs={{4,0},{8,12},{5,1},{9,13},{6,2},{10,14},{7,3},{11,15},{20,16},{24,... | collective-permute-start | bytes 3735560 | tf_op jit(solution)/shard_map/ppermute | solution.py:47
  150.1 3.9 %slice-start = ((s8[5242880]{0:T(1024)(128)(4,1)}), s8[4194304]{0:T(1024)(128)(4,1)S(1)}, s32[]{:S(2)}) async-start(s8[5242880]{0:T(1024)(128)(4,1)} %bitcast.16), calls=%async_computation | async-start | bytes 8388608
  150.1 21.1 %slice-start.2 = ((s8[4980736]{0:T(1024)(128)(4,1)}), s8[4194304]{0:T(1024)(128)(4,1)S(1)}, s32[]{:S(2)}) async-start(s8[4980736]{0:T(1024)(128)(4,1)} %bitcast.18), calls=%async_computation.2 | async-start | bytes 8388608
  150.2 4.8 %slice-start.1 = ((s8[5242880]{0:T(1024)(128)(4,1)}), s8[1048576]{0:T(1024)(128)(4,1)S(1)}, s32[]{:S(2)}) async-start(s8[5242880]{0:T(1024)(128)(4,1)} %bitcast.16), calls=%async_computation.1 | async-start | bytes 2097152
  150.2 21.1 %slice-start.3 = ((s8[4980736]{0:T(1024)(128)(4,1)}), s8[786432]{0:T(1024)(128)(4,1)S(1)}, s32[]{:S(2)}) async-start(s8[4980736]{0:T(1024)(128)(4,1)} %bitcast.18), calls=%async_computation.3 | async-start | bytes 1572864
  168.7 49.3 %collective-permute-start.7 = (bf16[152,2048]{1,0:T(8,128)(2,1)S(1)}, bf16[152,2048]{1,0:T(8,128)(2,1)S(1)}, u32[]{:S(2)}, u32[]{:S(2)}) collective-permute-start(bf16[152,2048]{1,0:T(8,128)(2,1)S(1)} %slice.61), channel_id=1, source_target_pairs={{4,8},{8,4},{5,9},{9,5},{6,10},{10,6},{7,11},{11,7},{20,24},{24,20... | collective-permute-start | bytes 1867784 | tf_op jit(solution)/shard_map/ppermute | solution.py:47
  230.2 1.9 collective-permute-start.9
  232.2 6.1 %collective-permute-start.10 = (f32[152,160]{1,0:T(8,128)S(1)}, f32[152,160]{1,0:T(8,128)S(1)}, u32[]{:S(2)}, u32[]{:S(2)}) collective-permute-start(f32[152,160]{1,0:T(8,128)S(1)} %get-tuple-element.19), channel_id=1, source_target_pairs={{0,2},{1,3},{2,0},{3,1},{4,6},{5,7},{6,4},{7,5},{8,10},{9,11},{10,... | collective-permute-start | bytes 291848 | tf_op jit(solution)/shard_map/ppermute | solution.py:109
  232.8 5.5 %collective-permute-start.12 = (f32[152,160]{1,0:T(8,128)S(1)}, f32[152,160]{1,0:T(8,128)S(1)}, u32[]{:S(2)}, u32[]{:S(2)}) collective-permute-start(f32[152,160]{1,0:T(8,128)S(1)} %get-tuple-element.20), channel_id=1, source_target_pairs={{6,2},{7,3},{10,14},{11,13},{22,18},{23,19},{26,30},{27,29}} | collective-permute-start | bytes 291848 | tf_op jit(solution)/shard_map/ppermute | solution.py:111
  234.1 4.3 %collective-permute-start.11 = (f32[152,160]{1,0:T(8,128)S(1)}, f32[152,160]{1,0:T(8,128)S(1)}, u32[]{:S(2)}, u32[]{:S(2)}) collective-permute-start(f32[152,160]{1,0:T(8,128)S(1)} %get-tuple-element.20), channel_id=1, source_target_pairs={{4,2},{5,3},{8,14},{9,13},{20,18},{21,19},{24,30},{25,29}} | collective-permute-start | bytes 291848 | tf_op jit(solution)/shard_map/ppermute | solution.py:110

commit v2 on v1

v2 whole, which is shorter than its diff:
```python
import jax
import jax.numpy as jnp
from jax import lax
from jax.sharding import PartitionSpec as P

WINDOW = 4
LINE = 4


def from_behind(value, axis, steps):
    count = lax.axis_size(axis)
    pairs = [(source, (source + steps) % count) for source in range(count)]
    return lax.ppermute(value, axis, pairs)


def products(rows, docs):
    return lax.dot_general(
        rows, docs, (((1,), (1,)), ((), ())), preferred_element_type=jnp.float32
    )


def ring(queries, store):
    blocks = [queries]
    for _ in range(WINDOW - 1):
        blocks.append(from_behind(blocks[-1], "docs", -1))
    return lax.psum_scatter(
        products(jnp.concatenate(blocks, axis=0), store),
        "proj",
        scatter_dimension=0,
        tiled=True,
    )


def after(value, *others):
    return lax.optimization_barrier((value,) + others)[0]


ENDS = [(0, 1), (1, 0), (2, 3), (3, 2)]
MIDDLE = [(1, 2), (2, 1)]
OUTWARD = [(1, 0), (2, 3)]
INWARD = [(0, 1), (3, 2)]
CORES = [(0, 1), (1, 0), (2, 3), (3, 2)]
CHIPS = [(0, 2), (1, 3), (2, 0), (3, 1)]


def along(value, pairs):
    return lax.ppermute(value, "docs", pairs)


def across(value, pairs):
    parts = lax.axis_size("proj")
    return lax.ppermute(
        value, ("docs", "proj"), [(a * parts + b, c * parts + d) for a, b, c, d in pairs]
    )


def line(queries, store):
    depth = queries.shape[1]
    cut = depth * 11 // 32 // 128 * 128
    start = depth // 16 // 128 * 128
    last = depth * 13 // 16 // 128 * 128 - cut
    first, body, tail = slice(0, start), slice(start, last), slice(last, None)
    place = lax.axis_index("docs")
    share = lax.axis_index("proj")
    inner = (place == 1) | (place == 2)
    left = place < 2
    even = share % 2 == 0
    low = share < 2
    near_store, far_store = store[:, :cut], store[:, cut:]

    middle = along(queries, MIDDLE)
    ends_near = along(queries[:, :cut], ENDS)
    ends_rest = along(after(queries[:, cut:], ends_near, far_store), ENDS)
    far_near = along(ends_near, MIDDLE)
    relayed = along(middle[:, :cut], OUTWARD)
    far_first = along(after(ends_rest[:, first], middle), MIDDLE)
    outer_store = along(after(far_store, middle), INWARD)
    far_body = along(after(ends_rest[:, body], middle), MIDDLE)
    far_relayed = along(after(far_near, relayed, far_first), OUTWARD)
    far_tail = along(after(ends_rest[:, tail], far_relayed, far_first), MIDDLE)

    own_part = products(queries, store)
    ends_part = products(ends_near, near_store) + products(ends_rest, far_store)
    middle_part = products(middle, store) + products(relayed, near_store)
    zeros = jnp.zeros_like(own_part)
    second = jnp.where(inner & left, middle_part, jnp.where(inner | left, ends_part, zeros))
    third = jnp.where(inner, zeros, middle_part)
    fourth = jnp.where(left, jnp.where(inner, ends_part, zeros), jnp.where(inner, middle_part, ends_part))
    kept = jnp.concatenate([jnp.where(even, own_part, second), jnp.where(even, third, fourth)], axis=0)
    given = jnp.concatenate([jnp.where(even, second, own_part), jnp.where(even, fourth, third)], axis=0)
    kept = kept + lax.ppermute(given, "proj", CORES)
    rows = queries.shape[0]
    early = jnp.where(low, kept[:rows], kept[rows:]) + lax.ppermute(
        jnp.where(low, kept[rows:], kept[:rows]), "proj", CHIPS
    )

    helped = products(middle[:, cut:], outer_store)
    helped = helped + lax.ppermute(helped, "proj", [(1, 0), (3, 2)])
    helped_one = across(helped, [(1, 0, 0, 2), (2, 0, 3, 2)])
    helped_two = across(helped, [(1, 2, 0, 2), (2, 2, 3, 2)])

    far_body = after(far_body, far_relayed)
    for_inner = (
        products(far_near, near_store)
        + products(far_first, far_store[:, first])
        + products(far_body, far_store[:, body])
    )
    for_outer = (
        products(far_relayed, near_store)
        + products(far_first, outer_store[:, first])
        + products(far_body, outer_store[:, body])
    )
    kept = jnp.where(even, for_inner, for_outer)
    given = jnp.where(even, for_outer, for_inner)
    kept_store = jnp.where(even, far_store[:, tail], outer_store[:, tail])
    given_store = jnp.where(even, outer_store[:, tail], far_store[:, tail])
    kept, given, kept_store, given_store, early, helped_one, helped_two = lax.optimization_barrier(
        (kept, given, kept_store, given_store, early, helped_one, helped_two)
    )
    given = given + products(far_tail, given_store)
    kept = kept + products(far_tail, kept_store)
    kept = kept + lax.ppermute(given, "proj", CORES)
    one = across(kept, [(1, 0, 1, 2), (2, 0, 2, 2), (1, 1, 0, 3), (2, 3, 3, 1)])
    two = across(kept, [(1, 3, 0, 3), (2, 1, 3, 1)])
    three = across(kept, [(0, 1, 0, 3), (3, 3, 3, 1)])
    stays = jnp.where(share == jnp.where(inner, 2, jnp.where(left, 3, 1)), kept, 0.0)
    return early + helped_one + helped_two + stays + one + two + three


def per_device(queries, store):
    if lax.axis_size("docs") == LINE and lax.axis_size("proj") == WINDOW:
        return line(queries, store)
    return ring(queries, store)


def solution(mesh):
    placed = (P(("groups", "docs"), "proj"), P(("groups", "docs"), "proj"))
    return jax.shard_map(
        per_device,
        mesh=mesh,
        in_specs=placed,
        out_specs=P("proj", ("groups", "docs")),
        check_vma=False,
    )
```

time: 243 us -> 236 us (0.971)
  waiting for transfers between devices: 178 us -> 154 us
  matrix products: 25.5 us -> 31.4 us
  starting transfers between devices: 22.2 us -> 28 us
  other arithmetic: 0.93 us -> 4.87 us
    ppermute x9 -> x10, waiting for transfers between devices: 172 us -> 143 us  [along(): return lax.ppermute(value, 'docs', pairs)]
    slice x3 -> x4, local copies, waits for them, and re-layouts: 2.56 us -> 9.34 us  [the longest x1 3.95 us: line(): ends_rest = along(after(queries[:, cut:], ends_near, far_store), ENDS)]
    dot_general x12 -> x14, matrix products: 25.5 us -> 31.4 us  [products(): lax.dot_general(rows, docs, (((1,), (1,)), ((), ())), preferred_element_t...]
    ppermute x4 -> x9, waiting for transfers between devices: 5.38 us -> 11.2 us  [the longest x5 5.8 us: across(): lax.ppermute(value, ('docs', 'proj'), [(a * parts + b, c * parts + d) for...]
    ppermute x4 -> x9, starting transfers between devices: 2.62 us -> 7.08 us  [the longest x5 4.6 us: across(): lax.ppermute(value, ('docs', 'proj'), [(a * parts + b, c * parts + d) for...]
    slice x1, local copies, waits for them, and re-layouts: 4.39 us -> 0.24 us  [line(): near_store, far_store = (store[:, :cut], store[:, cut:])]
    unnamed x14 -> x24, local copies, waits for them, and re-layouts: 2.88 us -> 0.06 us
    ppermute x9 -> x10, starting transfers between devices: 19.6 us -> 20.9 us  [along(): return lax.ppermute(value, 'docs', pairs)]
  transfers between devices with their start and end apart: 13 -> 19, of which waited for: 8 -> 10; matrix products, arithmetic and copies ran while one was open for 13% -> 21% of each run, Pallas kernels for 0% -> 0%
where the time goes in v2:
time: 236 us; the launch traced here: 231 us
  waiting for transfers between devices  154 us (65%)
  matrix products  31.4 us (13%)
  starting transfers between devices  28 us (12%)
  local copies, waits for them, and re-layouts  12.7 us (5%)
  other arithmetic  4.87 us (2%)
    ppermute x10, waiting for transfers between devices, along(): return lax.ppermute(value, 'docs', pairs)  143 us
    dot_general x14, matrix products, products(): lax.dot_general(rows, docs, (((1,), (1,)), ((), ())), preferred_element_t...  31.4 us
    ppermute x10, starting transfers between devices, along(): return lax.ppermute(value, 'docs', pairs)  20.9 us
    ppermute x5, waiting for transfers between devices, across(): lax.ppermute(value, ('docs', 'proj'), [(a * parts + b, c * parts + d) for...  5.8 us
  transfers between devices with their start and end apart: 19, of which 10 were waited for; matrix products, arithmetic and copies ran while one was open for 21% of the time, Pallas kernels for 0%

profile of v2, /device:TPU:18, one launch (start us, length us, event | category | flops | bytes accessed | tf_op | source)
XLA Modules:
  0.0 231.3 jit_solution(17037202087784658520)
XLA Ops:
  0.0 2.3 %collective-permute-start.3 = (bf16[152,16384]{1,0:T(8,128)(2,1)}, bf16[152,16384]{1,0:T(8,128)(2,1)S(1)}, u32[]{:S(2)}, u32[]{:S(2)}) collective-permute-start(bf16[152,16384]{1,0:T(8,128)(2,1)} %param.2), channel_id=1, source_target_pairs={{4,8},{8,4},{5,9},{9,5},{6,10},{10,6},{7,11},{11,7},{20,24},{24,20... | collective-permute-start | bytes 14942216 | tf_op jit(solution)/shard_map/ppermute | solution.py:47
  2.4 1.6 slice.58
  4.2 4.0 %slice.60 = bf16[152,10752]{1,0:T(8,128)(2,1)} slice(bf16[152,16384]{1,0:T(8,128)(2,1)} %param.2), slice={[0:152], [5632:16384]} | slice | bytes 6537216 | tf_op jit(solution)/shard_map/slice | solution.py:73
  8.4 34.6 %collective-permute-done = bf16[152,5632]{1,0:T(8,128)(2,1)} collective-permute-done((bf16[152,5632]{1,0:T(8,128)(2,1)S(1)}, bf16[152,5632]{1,0:T(8,128)(2,1)}, u32[]{:S(2)}, u32[]{:S(2)}) %collective-permute-start) | collective-permute-done | bytes 1712160 | tf_op jit(solution)/shard_map/ppermute | solution.py:47
  43.4 3.3 %collective-permute-start.1 = (bf16[152,5632]{1,0:T(8,128)(2,1)}, bf16[152,5632]{1,0:T(8,128)(2,1)}, u32[]{:S(2)}, u32[]{:S(2)}) collective-permute-start(bf16[152,5632]{1,0:T(8,128)(2,1)} %collective-permute-done), channel_id=1, source_target_pairs={{4,8},{8,4},{5,9},{9,5},{6,10},{10,6},{7,11},{11,7},{20,24},{24,20... | collective-permute-start | bytes 5136392 | tf_op jit(solution)/shard_map/ppermute | solution.py:47
  46.7 65.7 %collective-permute-done.3 = bf16[152,16384]{1,0:T(8,128)(2,1)S(1)} collective-permute-done((bf16[152,16384]{1,0:T(8,128)(2,1)}, bf16[152,16384]{1,0:T(8,128)(2,1)S(1)}, u32[]{:S(2)}, u32[]{:S(2)}) %collective-permute-start.3) | collective-permute-done | bytes 4980768 | tf_op jit(solution)/shard_map/ppermute | solution.py:47
  112.4 1.5 slice.77
  113.9 2.5 %collective-permute-start.6 = (bf16[152,5632]{1,0:T(8,128)(2,1)}, bf16[152,5632]{1,0:T(8,128)(2,1)}, u32[]{:S(2)}, u32[]{:S(2)}) collective-permute-start(bf16[152,5632]{1,0:T(8,128)(2,1)} %slice.77), channel_id=1, source_target_pairs={{4,0},{8,12},{5,1},{9,13},{6,2},{10,14},{7,3},{11,15},{20,16},{24,... | collective-permute-start | bytes 5136392 | tf_op jit(solution)/shard_map/ppermute | solution.py:47
  116.4 1.3 collective-permute-start.8
  117.7 2.5 %fusion.38 = f32[152,160]{1,0:T(8,128)} fusion(bf16[152,16384]{1,0:T(8,128)(2,1)S(1)} %bitcast.21, bf16[160,16384]{1,0:T(8,128)(2,1)S(1)} %copy-done), kind=kOutput, calls=%fused_computation.43 | convolution fusion | flops 796917760 | bytes 10320896 | tf_op jit(solution)/shard_map/dot_general | solution.py:17
  120.2 3.2 %slice.76 = bf16[152,6656]{1,0:T(8,128)(2,1)} slice(bf16[152,10752]{1,0:T(8,128)(2,1)} %collective-permute-done.2), slice={[0:152], [1024:7680]} | slice | bytes 4046848 | tf_op jit(solution)/shard_map/slice | solution.py:78
  123.3 1.0 slice.75
  124.3 2.5 %collective-permute-start.4 = (bf16[152,1024]{1,0:T(8,128)(2,1)S(1)}, bf16[152,1024]{1,0:T(8,128)(2,1)}, u32[]{:S(2)}, u32[]{:S(2)}) collective-permute-start(bf16[152,1024]{1,0:T(8,128)(2,1)S(1)} %slice.75), channel_id=1, source_target_pairs={{4,8},{8,4},{5,9},{9,5},{6,10},{10,6},{7,11},{11,7},{20,24},{24,20... | collective-permute-start | bytes 933896 | tf_op jit(solution)/shard_map/ppermute | solution.py:47
  126.8 3.5 %collective-permute-start.5 = (bf16[152,6656]{1,0:T(8,128)(2,1)}, bf16[152,6656]{1,0:T(8,128)(2,1)}, u32[]{:S(2)}, u32[]{:S(2)}) collective-permute-start(bf16[152,6656]{1,0:T(8,128)(2,1)} %slice.76), channel_id=1, source_target_pairs={{4,8},{8,4},{5,9},{9,5},{6,10},{10,6},{7,11},{11,7},{20,24},{24,20... | collective-permute-start | bytes 6070280 | tf_op jit(solution)/shard_map/ppermute | solution.py:47
  130.3 4.2 %fusion.36 = f32[152,160]{1,0:T(8,128)S(1)} fusion(bf16[152,10752]{1,0:T(8,128)(2,1)} %collective-permute-done.2, bf16[160,16384]{1,0:T(8,128)(2,1)} %param.3), kind=kOutput, calls=%fused_computation.41 | convolution fusion | flops 522977280 | bytes 6806528 | tf_op jit(solution)/shard_map/dot_general | solution.py:17
  134.5 2.2 fusion.29
  136.7 12.5 %collective-permute-done.1 = bf16[152,5632]{1,0:T(8,128)(2,1)} collective-permute-done((bf16[152,5632]{1,0:T(8,128)(2,1)}, bf16[152,5632]{1,0:T(8,128)(2,1)}, u32[]{:S(2)}, u32[]{:S(2)}) %collective-permute-start.1) | collective-permute-done | bytes 1712160 | tf_op jit(solution)/shard_map/ppermute | solution.py:47
  149.2 6.7 %collective-permute-done.4 = bf16[152,1024]{1,0:T(8,128)(2,1)} collective-permute-done((bf16[152,1024]{1,0:T(8,128)(2,1)S(1)}, bf16[152,1024]{1,0:T(8,128)(2,1)}, u32[]{:S(2)}, u32[]{:S(2)}) %collective-permute-start.4) | collective-permute-done | bytes 311328 | tf_op jit(solution)/shard_map/ppermute | solution.py:47
  155.9 2.5 %collective-permute-start.7 = (bf16[152,5632]{1,0:T(8,128)(2,1)}, bf16[152,5632]{1,0:T(8,128)(2,1)}, u32[]{:S(2)}, u32[]{:S(2)}) collective-permute-start(bf16[152,5632]{1,0:T(8,128)(2,1)} %collective-permute-done.1), channel_id=1, source_target_pairs={{4,0},{8,12},{5,1},{9,13},{6,2},{10,14},{7,3},{11,15},{20,16},{24,... | collective-permute-start | bytes 5136392 | tf_op jit(solution)/shard_map/ppermute | solution.py:47
  158.4 2.1 fusion.8
  160.5 2.5 %broadcast_select_fusion.3 = (f32[152,160]{1,0:T(8,128)}, f32[152,160]{1,0:T(8,128)S(1)}, f32[152,160]{1,0:T(8,128)}, f32[152,160]{1,0:T(8,128)S(1)}) fusion(f32[152,160]{1,0:T(8,128)S(1)} %copy-done.3, pred[]{:T(512)S(6)} %eq.14, f32[152,160]{1,0:T(8,128)S(1)} %fusion.29, pred[]{:T(512)S(6)} %or.7, pred[]{:T(512)S(6)} %and.11, pred[]{:T(512)S(6)} %lt.14, ...), kind=kOutput, calls=%fused_computation.38 | convolution fusion | flops 797185280 | bytes 10904581 | tf_op jit(solution)/shard_map/dot_general | solution.py:17
  163.0 0.8 pad_maximum_fusion
  163.7 1.2 slice.84
  165.0 0.7 collective-permute-done.9
  165.7 1.1 maximum_add_fusion
  166.8 0.6 collective-permute-start.10
  167.4 1.3 fusion.34
  168.8 4.2 %collective-permute-done.10 = f32[152,160]{1,0:T(8,128)S(1)} collective-permute-done((f32[152,160]{1,0:T(8,128)S(1)}, f32[152,160]{1,0:T(8,128)S(1)}, u32[]{:S(2)}, u32[]{:S(2)}) %collective-permute-start.10) | collective-permute-done | bytes 97312 | tf_op jit(solution)/shard_map/ppermute | solution.py:93
  173.0 0.7 select_add_fusion
  173.7 18.7 %collective-permute-done.7 = bf16[152,5632]{1,0:T(8,128)(2,1)} collective-permute-done((bf16[152,5632]{1,0:T(8,128)(2,1)}, bf16[152,5632]{1,0:T(8,128)(2,1)}, u32[]{:S(2)}, u32[]{:S(2)}) %collective-permute-start.7) | collective-permute-done | bytes 1712160 | tf_op jit(solution)/shard_map/ppermute | solution.py:47
  192.4 2.3 %collective-permute-start.14 = (bf16[152,3072]{1,0:T(8,128)(2,1)S(1)}, bf16[152,3072]{1,0:T(8,128)(2,1)S(1)}, u32[]{:S(2)}, u32[]{:S(2)}) collective-permute-start(bf16[152,3072]{1,0:T(8,128)(2,1)S(1)} %slice.84), channel_id=1, source_target_pairs={{4,8},{8,4},{5,9},{9,5},{6,10},{10,6},{7,11},{11,7},{20,24},{24,20... | collective-permute-start | bytes 2801672 | tf_op jit(solution)/shard_map/ppermute | solution.py:47
  194.7 4.5 %collective-permute-done.5 = bf16[152,6656]{1,0:T(8,128)(2,1)} collective-permute-done((bf16[152,6656]{1,0:T(8,128)(2,1)}, bf16[152,6656]{1,0:T(8,128)(2,1)}, u32[]{:S(2)}, u32[]{:S(2)}) %collective-permute-start.5) | collective-permute-done | bytes 2023456 | tf_op jit(solution)/shard_map/ppermute | solution.py:47
  199.2 3.1 %fusion.4 = f32[152,160]{1,0:T(8,128)S(1)} fusion(bf16[152,6656]{1,0:T(8,128)(2,1)} %collective-permute-done.5, bf16[160,16384]{1,0:T(8,128)(2,1)} %param.3), kind=kOutput, calls=%fused_computation.4 | convolution fusion | flops 323747840 | bytes 4250624 | tf_op jit(solution)/shard_map/dot_general | solution.py:17
  202.3 4.1 %fusion.14 = f32[152,160]{1,0:T(8,128)S(1)} fusion(bf16[160,10752]{1,0:T(8,128)(2,1)} %collective-permute-done.8, bf16[152,16384]{1,0:T(8,128)(2,1)} %copy-done.2), kind=kOutput, calls=%fused_computation.14 | convolution fusion | flops 522977280 | bytes 6806528 | tf_op jit(solution)/shard_map/dot_general | solution.py:17
  206.5 1.3 collective-permute-start.11
  207.8 1.5 broadcast_select_fusion
  209.3 2.9 %fusion.2 = f32[152,160]{1,0:T(8,128)S(1)} fusion(bf16[152,6656]{1,0:T(8,128)(2,1)} %collective-permute-done.5, bf16[160,10752]{1,0:T(8,128)(2,1)} %collective-permute-done.8), kind=kOutput, calls=%fused_computation.2 | convolution fusion | flops 323747840 | bytes 4250624 | tf_op jit(solution)/shard_map/dot_general | solution.py:17
  212.2 1.3 fusion.32
  213.5 2.2 fusion.26
  215.7 1.3 collective-permute-start.13
  217.0 0.7 collective-permute-start.12
  217.7 2.2 broadcast_select_fusion.4
  220.4 0.6 collective-permute-start.15
  222.1 0.7 collective-permute-start.18
  222.7 0.7 collective-permute-start.17
  223.4 1.3 collective-permute-start.16
  224.7 5.8 %collective-permute-done.16 = f32[152,160]{1,0:T(8,128)S(1)} collective-permute-done((f32[152,160]{1,0:T(8,128)S(1)}, f32[152,160]{1,0:T(8,128)S(1)}, u32[]{:S(2)}, u32[]{:S(2)}) %collective-permute-start.16) | collective-permute-done | bytes 97312 | tf_op jit(solution)/shard_map/ppermute | solution.py:52
  230.5 0.8 add_add_fusion
  (48 shorter events, 2.6 us)
Async XLA Ops:
  0.0 112.4 %collective-permute-start.3 = (bf16[152,16384]{1,0:T(8,128)(2,1)}, bf16[152,16384]{1,0:T(8,128)(2,1)S(1)}, u32[]{:S(2)}, u32[]{:S(2)}) collective-permute-start(bf16[152,16384]{1,0:T(8,128)(2,1)} %param.2), channel_id=1, source_target_pairs={{4,8},{8,4},{5,9},{9,5},{6,10},{10,6},{7,11},{11,7},{20,24},{24,20... | collective-permute-start | bytes 14942216 | tf_op jit(solution)/shard_map/ppermute | solution.py:47
  3.9 4.2 %copy-start = (bf16[160,16384]{1,0:T(8,128)(2,1)S(1)}, bf16[160,16384]{1,0:T(8,128)(2,1)}, u32[]{:S(2)}) copy-start(bf16[160,16384]{1,0:T(8,128)(2,1)} %param.3) | copy-start | bytes 15728644
  3.9 39.0 %collective-permute-start = (bf16[152,5632]{1,0:T(8,128)(2,1)S(1)}, bf16[152,5632]{1,0:T(8,128)(2,1)}, u32[]{:S(2)}, u32[]{:S(2)}) collective-permute-start(bf16[152,5632]{1,0:T(8,128)(2,1)S(1)} %slice.58), channel_id=1, source_target_pairs={{0,4},{4,0},{8,12},{12,8},{1,5},{5,1},{9,13},{13,9},{2,6},{6,2},{1... | collective-permute-start | bytes 5136392 | tf_op jit(solution)/shard_map/ppermute | solution.py:47
  4.2 113.5 %slice-start = ((s8[4980736]{0:T(1024)(128)(4,1)}), s8[4194304]{0:T(1024)(128)(4,1)S(1)}, s32[]{:S(2)}) async-start(s8[4980736]{0:T(1024)(128)(4,1)} %bitcast.20), calls=%async_computation | async-start | bytes 8388608
  8.2 109.5 %slice-start.1 = ((s8[4980736]{0:T(1024)(128)(4,1)}), s8[786432]{0:T(1024)(128)(4,1)S(1)}, s32[]{:S(2)}) async-start(s8[4980736]{0:T(1024)(128)(4,1)} %bitcast.20), calls=%async_computation.1 | async-start | bytes 1572864
  43.0 77.2 %collective-permute-start.2 = (bf16[152,10752]{1,0:T(8,128)(2,1)}, bf16[152,10752]{1,0:T(8,128)(2,1)}, u32[]{:S(2)}, u32[]{:S(2)}) collective-permute-start(bf16[152,10752]{1,0:T(8,128)(2,1)} %slice.60), channel_id=1, source_target_pairs={{0,4},{4,0},{8,12},{12,8},{1,5},{5,1},{9,13},{13,9},{2,6},{6,2},{1... | collective-permute-start | bytes 9805832 | tf_op jit(solution)/shard_map/ppermute | solution.py:47
  43.4 105.8 %collective-permute-start.1 = (bf16[152,5632]{1,0:T(8,128)(2,1)}, bf16[152,5632]{1,0:T(8,128)(2,1)}, u32[]{:S(2)}, u32[]{:S(2)}) collective-permute-start(bf16[152,5632]{1,0:T(8,128)(2,1)} %collective-permute-done), channel_id=1, source_target_pairs={{4,8},{8,4},{5,9},{9,5},{6,10},{10,6},{7,11},{11,7},{20,24},{24,20... | collective-permute-start | bytes 5136392 | tf_op jit(solution)/shard_map/ppermute | solution.py:47
  112.4 7.7 %copy-start.2 = (bf16[152,16384]{1,0:T(8,128)(2,1)}, bf16[152,16384]{1,0:T(8,128)(2,1)S(1)}, u32[]{:S(2)}) copy-start(bf16[152,16384]{1,0:T(8,128)(2,1)S(1)} %collective-permute-done.3) | copy-start | bytes 14942212
  113.9 42.0 %collective-permute-start.6 = (bf16[152,5632]{1,0:T(8,128)(2,1)}, bf16[152,5632]{1,0:T(8,128)(2,1)}, u32[]{:S(2)}, u32[]{:S(2)}) collective-permute-start(bf16[152,5632]{1,0:T(8,128)(2,1)} %slice.77), channel_id=1, source_target_pairs={{4,0},{8,12},{5,1},{9,13},{6,2},{10,14},{7,3},{11,15},{20,16},{24,... | collective-permute-start | bytes 5136392 | tf_op jit(solution)/shard_map/ppermute | solution.py:47
  116.4 86.0 %collective-permute-start.8 = (bf16[160,10752]{1,0:T(8,128)(2,1)S(1)}, bf16[160,10752]{1,0:T(8,128)(2,1)}, u32[]{:S(2)}, u32[]{:S(2)}) collective-permute-start(bf16[160,10752]{1,0:T(8,128)(2,1)S(1)} %slice.61), channel_id=1, source_target_pairs={{0,4},{12,8},{1,5},{13,9},{2,6},{14,10},{3,7},{15,11},{16,20},{28,... | collective-permute-start | bytes 10321928 | tf_op jit(solution)/shard_map/ppermute | solution.py:47
  120.1 14.4 %slice-start.2 = ((s8[5242880]{0:T(1024)(128)(4,1)}), s8[4194304]{0:T(1024)(128)(4,1)S(1)}, s32[]{:S(2)}) async-start(s8[5242880]{0:T(1024)(128)(4,1)} %bitcast.22), calls=%async_computation.2 | async-start | bytes 8388608
  124.3 10.2 %slice-start.3 = ((s8[5242880]{0:T(1024)(128)(4,1)}), s8[1048576]{0:T(1024)(128)(4,1)S(1)}, s32[]{:S(2)}) async-start(s8[5242880]{0:T(1024)(128)(4,1)} %bitcast.22), calls=%async_computation.3 | async-start | bytes 2097152
  124.3 31.6 %collective-permute-start.4 = (bf16[152,1024]{1,0:T(8,128)(2,1)S(1)}, bf16[152,1024]{1,0:T(8,128)(2,1)}, u32[]{:S(2)}, u32[]{:S(2)}) collective-permute-start(bf16[152,1024]{1,0:T(8,128)(2,1)S(1)} %slice.75), channel_id=1, source_target_pairs={{4,8},{8,4},{5,9},{9,5},{6,10},{10,6},{7,11},{11,7},{20,24},{24,20... | collective-permute-start | bytes 933896 | tf_op jit(solution)/shard_map/ppermute | solution.py:47
  126.8 72.4 %collective-permute-start.5 = (bf16[152,6656]{1,0:T(8,128)(2,1)}, bf16[152,6656]{1,0:T(8,128)(2,1)}, u32[]{:S(2)}, u32[]{:S(2)}) collective-permute-start(bf16[152,6656]{1,0:T(8,128)(2,1)} %slice.76), channel_id=1, source_target_pairs={{4,8},{8,4},{5,9},{9,5},{6,10},{10,6},{7,11},{11,7},{20,24},{24,20... | collective-permute-start | bytes 6070280 | tf_op jit(solution)/shard_map/ppermute | solution.py:47
  130.3 30.2 %slice-start.6 = ((s8[4980736]{0:T(1024)(128)(4,1)}), s8[4194304]{0:T(1024)(128)(4,1)S(1)}, s32[]{:S(2)}) async-start(s8[4980736]{0:T(1024)(128)(4,1)} %bitcast.26), calls=%async_computation.6 | async-start | bytes 8388608
  134.5 26.0 %slice-start.7 = ((s8[4980736]{0:T(1024)(128)(4,1)}), s8[786432]{0:T(1024)(128)(4,1)S(1)}, s32[]{:S(2)}) async-start(s8[4980736]{0:T(1024)(128)(4,1)} %bitcast.26), calls=%async_computation.7 | async-start | bytes 1572864
  136.7 23.8 %copy-start.3 = (f32[152,160]{1,0:T(8,128)S(1)}, f32[152,160]{1,0:T(8,128)}, u32[]{:S(2)}) copy-start(f32[152,160]{1,0:T(8,128)} %fusion.38) | copy-start | bytes 291844
  155.9 36.5 %collective-permute-start.7 = (bf16[152,5632]{1,0:T(8,128)(2,1)}, bf16[152,5632]{1,0:T(8,128)(2,1)}, u32[]{:S(2)}, u32[]{:S(2)}) collective-permute-start(bf16[152,5632]{1,0:T(8,128)(2,1)} %collective-permute-done.1), channel_id=1, source_target_pairs={{4,0},{8,12},{5,1},{9,13},{6,2},{10,14},{7,3},{11,15},{20,16},{24,... | collective-permute-start | bytes 5136392 | tf_op jit(solution)/shard_map/ppermute | solution.py:47
  163.7 1.9 collective-permute-start.9
  166.8 6.1 %collective-permute-start.10 = (f32[152,160]{1,0:T(8,128)S(1)}, f32[152,160]{1,0:T(8,128)S(1)}, u32[]{:S(2)}, u32[]{:S(2)}) collective-permute-start(f32[152,160]{1,0:T(8,128)S(1)} %slice_select_fusion), channel_id=1, source_target_pairs={{0,2},{1,3},{2,0},{3,1},{4,6},{5,7},{6,4},{7,5},{8,10},{9,11},{10,... | collective-permute-start | bytes 291848 | tf_op jit(solution)/shard_map/ppermute | solution.py:93
  192.4 27.5 %collective-permute-start.14 = (bf16[152,3072]{1,0:T(8,128)(2,1)S(1)}, bf16[152,3072]{1,0:T(8,128)(2,1)S(1)}, u32[]{:S(2)}, u32[]{:S(2)}) collective-permute-start(bf16[152,3072]{1,0:T(8,128)(2,1)S(1)} %slice.84), channel_id=1, source_target_pairs={{4,8},{8,4},{5,9},{9,5},{6,10},{10,6},{7,11},{11,7},{20,24},{24,20... | collective-permute-start | bytes 2801672 | tf_op jit(solution)/shard_map/ppermute | solution.py:47
  199.2 8.5 %slice-start.4 = ((s8[5242880]{0:T(1024)(128)(4,1)}), s8[4194304]{0:T(1024)(128)(4,1)S(1)}, s32[]{:S(2)}) async-start(s8[5242880]{0:T(1024)(128)(4,1)} %bitcast.24), calls=%async_computation.4 | async-start | bytes 8388608
  202.3 5.5 %slice-start.5 = ((s8[5242880]{0:T(1024)(128)(4,1)}), s8[1048576]{0:T(1024)(128)(4,1)S(1)}, s32[]{:S(2)}) async-start(s8[5242880]{0:T(1024)(128)(4,1)} %bitcast.24), calls=%async_computation.5 | async-start | bytes 2097152
  206.5 9.2 %collective-permute-start.11 = (f32[152,160]{1,0:T(8,128)S(1)}, f32[152,160]{1,0:T(8,128)S(1)}, u32[]{:S(2)}, u32[]{:S(2)}) collective-permute-start(f32[152,160]{1,0:T(8,128)S(1)} %fusion.14), channel_id=1, source_target_pairs={{1,0},{3,2},{5,4},{7,6},{9,8},{11,10},{13,12},{15,14},{17,16},{19,... | collective-permute-start | bytes 291848 | tf_op jit(solution)/shard_map/ppermute | solution.py:98
  215.7 4.2 %collective-permute-start.13 = (f32[152,160]{1,0:T(8,128)S(1)}, f32[152,160]{1,0:T(8,128)S(1)}, u32[]{:S(2)}, u32[]{:S(2)}) collective-permute-start(f32[152,160]{1,0:T(8,128)S(1)} %add.67), channel_id=1, source_target_pairs={{6,2},{10,14},{22,18},{26,30}} | collective-permute-start | bytes 291848 | tf_op jit(solution)/shard_map/ppermute | solution.py:52
  217.0 2.9 %collective-permute-start.12 = (f32[152,160]{1,0:T(8,128)S(1)}, f32[152,160]{1,0:T(8,128)S(1)}, u32[]{:S(2)}, u32[]{:S(2)}) collective-permute-start(f32[152,160]{1,0:T(8,128)S(1)} %add.67), channel_id=1, source_target_pairs={{4,2},{8,14},{20,18},{24,30}} | collective-permute-start | bytes 291848 | tf_op jit(solution)/shard_map/ppermute | solution.py:52
  219.9 10.7 %copy-start.1 = (f32[152,160]{1,0:T(8,128)S(1)}, f32[152,160]{1,0:T(8,128)}, u32[]{:S(2)}) copy-start(f32[152,160]{1,0:T(8,128)} %select_add_fusion) | copy-start | bytes 291844
  220.4 1.6 collective-permute-start.15
  222.1 2.7 %collective-permute-start.18 = (f32[152,160]{1,0:T(8,128)S(1)}, f32[152,160]{1,0:T(8,128)S(1)}, u32[]{:S(2)}, u32[]{:S(2)}) collective-permute-start(f32[152,160]{1,0:T(8,128)S(1)} %add_add_fusion.1), channel_id=1, source_target_pairs={{1,3},{15,13},{17,19},{31,29}} | collective-permute-start | bytes 291848 | tf_op jit(solution)/shard_map/ppermute | solution.py:52
  222.7 2.0 collective-permute-start.17
  223.4 7.1 %collective-permute-start.16 = (f32[152,160]{1,0:T(8,128)S(1)}, f32[152,160]{1,0:T(8,128)S(1)}, u32[]{:S(2)}, u32[]{:S(2)}) collective-permute-start(f32[152,160]{1,0:T(8,128)S(1)} %add_add_fusion.1), channel_id=1, source_target_pairs={{4,6},{8,10},{5,3},{11,13},{20,22},{24,26},{21,19},{27,29}} | collective-permute-start | bytes 291848 | tf_op jit(solution)/shard_map/ppermute | solution.py:52

commit v3 on v2

--- a/solution.py
+++ b/solution.py
@@ -99,23 +99,23 @@
     helped_one = across(helped, [(1, 0, 0, 2), (2, 0, 3, 2)])
     helped_two = across(helped, [(1, 2, 0, 2), (2, 2, 3, 2)])
 
-    far_body = after(far_body, far_relayed)
-    for_inner = (
-        products(far_near, near_store)
-        + products(far_first, far_store[:, first])
-        + products(far_body, far_store[:, body])
-    )
+    for_inner = products(far_near, near_store) + products(far_first, far_store[:, first])
+    for_outer = products(far_relayed, near_store)
+    kept_store = jnp.where(even, far_store[:, tail], outer_store[:, tail])
+    given_store = jnp.where(even, outer_store[:, tail], far_store[:, tail])
+    far_body, for_inner, for_outer, kept_store, given_store = lax.optimization_barrier(
+        (far_body, for_inner, for_outer, kept_store, given_store, helped)
+    )[:5]
+    for_inner = for_inner + products(far_body, far_store[:, body])
     for_outer = (
-        products(far_relayed, near_store)
+        for_outer
         + products(far_first, outer_store[:, first])
         + products(far_body, outer_store[:, body])
     )
     kept = jnp.where(even, for_inner, for_outer)
     given = jnp.where(even, for_outer, for_inner)
-    kept_store = jnp.where(even, far_store[:, tail], outer_store[:, tail])
-    given_store = jnp.where(even, outer_store[:, tail], far_store[:, tail])
-    kept, given, kept_store, given_store, early, helped_one, helped_two = lax.optimization_barrier(
-        (kept, given, kept_store, given_store, early, helped_one, helped_two)
+    kept, given, kept_store, given_store, early = lax.optimization_barrier(
+        (kept, given, kept_store, given_store, early)
     )
     given = given + products(far_tail, given_store)
     kept = kept + products(far_tail, kept_store)

time: 236 us -> 230 us (0.975); the launches traced: 231 us -> 229 us
  waiting for transfers between devices: 154 us -> 168 us
  matrix products: 31.4 us -> 21.3 us
  other arithmetic: 4.87 us -> 1.12 us
    ppermute x10, waiting for transfers between devices: 143 us -> 155 us  [along(): return lax.ppermute(value, 'docs', pairs)]
    dot_general x14, matrix products: 31.4 us -> 21.3 us  [products(): lax.dot_general(rows, docs, (((1,), (1,)), ((), ())), preferred_element_t...]
  transfers between devices with their start and end apart: 19 -> 19, of which waited for: 10 -> 12; matrix products, arithmetic and copies ran while one was open for 21% -> 15% of each run, Pallas kernels for 0% -> 0%
where the time goes in v3:
time: 230 us; the launch traced here: 229 us
  waiting for transfers between devices  168 us (73%)
  starting transfers between devices  26.7 us (12%)
  matrix products  21.3 us (9%)
  local copies, waits for them, and re-layouts  11.8 us (5%)
    ppermute x10, waiting for transfers between devices, along(): return lax.ppermute(value, 'docs', pairs)  155 us
    dot_general x14, matrix products, products(): lax.dot_general(rows, docs, (((1,), (1,)), ((), ())), preferred_element_t...  21.3 us
    ppermute x10, starting transfers between devices, along(): return lax.ppermute(value, 'docs', pairs)  19.9 us
    ppermute x5, waiting for transfers between devices, across(): lax.ppermute(value, ('docs', 'proj'), [(a * parts + b, c * parts + d) for...  5.78 us
    ppermute x5, starting transfers between devices, across(): lax.ppermute(value, ('docs', 'proj'), [(a * parts + b, c * parts + d) for...  4.76 us
  transfers between devices with their start and end apart: 19, of which 12 were waited for; matrix products, arithmetic and copies ran while one was open for 15% of the time, Pallas kernels for 0%

profile of v3, /device:TPU:18, one launch (start us, length us, event | category | flops | bytes accessed | tf_op | source)
XLA Modules:
  0.0 229.2 jit_solution(5781518988986440192)
XLA Ops:
  0.0 2.3 %collective-permute-start.2 = (bf16[152,16384]{1,0:T(8,128)(2,1)}, bf16[152,16384]{1,0:T(8,128)(2,1)S(1)}, u32[]{:S(2)}, u32[]{:S(2)}) collective-permute-start(bf16[152,16384]{1,0:T(8,128)(2,1)} %param.2), channel_id=1, source_target_pairs={{4,8},{8,4},{5,9},{9,5},{6,10},{10,6},{7,11},{11,7},{20,24},{24,20... | collective-permute-start | bytes 14942216 | tf_op jit(solution)/shard_map/ppermute | solution.py:47
  2.4 1.6 slice.59
  4.2 3.9 %slice.58 = bf16[152,10752]{1,0:T(8,128)(2,1)} slice(bf16[152,16384]{1,0:T(8,128)(2,1)} %param.2), slice={[0:152], [5632:16384]} | slice | bytes 6537216 | tf_op jit(solution)/shard_map/slice | solution.py:73
  8.2 2.0 slice.60
  10.2 32.8 %collective-permute-done = bf16[152,5632]{1,0:T(8,128)(2,1)} collective-permute-done((bf16[152,5632]{1,0:T(8,128)(2,1)S(1)}, bf16[152,5632]{1,0:T(8,128)(2,1)}, u32[]{:S(2)}, u32[]{:S(2)}) %collective-permute-start) | collective-permute-done | bytes 1712160 | tf_op jit(solution)/shard_map/ppermute | solution.py:47
  43.0 0.5 collective-permute-start.1
  43.4 3.3 %collective-permute-start.4 = (bf16[152,5632]{1,0:T(8,128)(2,1)}, bf16[152,5632]{1,0:T(8,128)(2,1)}, u32[]{:S(2)}, u32[]{:S(2)}) collective-permute-start(bf16[152,5632]{1,0:T(8,128)(2,1)} %collective-permute-done), channel_id=1, source_target_pairs={{4,8},{8,4},{5,9},{9,5},{6,10},{10,6},{7,11},{11,7},{20,24},{24,20... | collective-permute-start | bytes 5136392 | tf_op jit(solution)/shard_map/ppermute | solution.py:47
  46.7 65.7 %collective-permute-done.2 = bf16[152,16384]{1,0:T(8,128)(2,1)S(1)} collective-permute-done((bf16[152,16384]{1,0:T(8,128)(2,1)}, bf16[152,16384]{1,0:T(8,128)(2,1)S(1)}, u32[]{:S(2)}, u32[]{:S(2)}) %collective-permute-start.2) | collective-permute-done | bytes 4980768 | tf_op jit(solution)/shard_map/ppermute | solution.py:47
  112.5 2.7 %collective-permute-start.6 = (bf16[152,5632]{1,0:T(8,128)(2,1)S(1)}, bf16[152,5632]{1,0:T(8,128)(2,1)}, u32[]{:S(2)}, u32[]{:S(2)}) collective-permute-start(bf16[152,5632]{1,0:T(8,128)(2,1)S(1)} %slice.77), channel_id=1, source_target_pairs={{4,0},{8,12},{5,1},{9,13},{6,2},{10,14},{7,3},{11,15},{20,16},{24,... | collective-permute-start | bytes 5136392 | tf_op jit(solution)/shard_map/ppermute | solution.py:47
  115.2 5.7 %fusion.29 = f32[152,160]{1,0:T(8,128)S(1)} fusion(bf16[152,16384]{1,0:T(8,128)(2,1)} %param.2, bf16[160,16384]{1,0:T(8,128)(2,1)} %param.3), kind=kOutput, calls=%fused_computation.41 | convolution fusion | flops 796917760 | bytes 10320896 | tf_op jit(solution)/shard_map/dot_general | solution.py:17
  120.9 1.1 slice.76
  122.1 1.7 slice.75
  123.8 2.4 %collective-permute-start.5 = (bf16[152,1024]{1,0:T(8,128)(2,1)S(1)}, bf16[152,1024]{1,0:T(8,128)(2,1)S(1)}, u32[]{:S(2)}, u32[]{:S(2)}) collective-permute-start(bf16[152,1024]{1,0:T(8,128)(2,1)S(1)} %slice.76), channel_id=1, source_target_pairs={{4,8},{8,4},{5,9},{9,5},{6,10},{10,6},{7,11},{11,7},{20,24},{24,20... | collective-permute-start | bytes 933896 | tf_op jit(solution)/shard_map/ppermute | solution.py:47
  126.1 3.5 %collective-permute-start.3 = (bf16[152,6656]{1,0:T(8,128)(2,1)S(1)}, bf16[152,6656]{1,0:T(8,128)(2,1)S(1)}, u32[]{:S(2)}, u32[]{:S(2)}) collective-permute-start(bf16[152,6656]{1,0:T(8,128)(2,1)S(1)} %slice.75), channel_id=1, source_target_pairs={{4,8},{8,4},{5,9},{9,5},{6,10},{10,6},{7,11},{11,7},{20,24},{24,20... | collective-permute-start | bytes 6070280 | tf_op jit(solution)/shard_map/ppermute | solution.py:47
  129.6 1.3 collective-permute-start.8
  130.9 1.2 slice.84
  132.2 3.1 %fusion.27 = f32[152,160]{1,0:T(8,128)S(1)} fusion(bf16[152,10752]{1,0:T(8,128)(2,1)} %collective-permute-done.1, bf16[160,16384]{1,0:T(8,128)(2,1)S(1)} %bitcast.21), kind=kOutput, calls=%fused_computation.39 | convolution fusion | flops 522977280 | bytes 6806528 | tf_op jit(solution)/shard_map/dot_general | solution.py:17
  135.4 2.2 fusion.20
  137.5 11.7 %collective-permute-done.4 = bf16[152,5632]{1,0:T(8,128)(2,1)} collective-permute-done((bf16[152,5632]{1,0:T(8,128)(2,1)}, bf16[152,5632]{1,0:T(8,128)(2,1)}, u32[]{:S(2)}, u32[]{:S(2)}) %collective-permute-start.4) | collective-permute-done | bytes 1712160 | tf_op jit(solution)/shard_map/ppermute | solution.py:47
  149.2 6.6 %collective-permute-done.5 = bf16[152,1024]{1,0:T(8,128)(2,1)S(1)} collective-permute-done((bf16[152,1024]{1,0:T(8,128)(2,1)S(1)}, bf16[152,1024]{1,0:T(8,128)(2,1)S(1)}, u32[]{:S(2)}, u32[]{:S(2)}) %collective-permute-start.5) | collective-permute-done | bytes 311328 | tf_op jit(solution)/shard_map/ppermute | solution.py:47
  155.8 1.4 collective-permute-start.7
  157.2 2.1 fusion.8
  159.3 1.6 broadcast_select_fusion.3
  161.0 0.3 fusion.25
  161.2 1.3 collective-permute-done.10
  162.6 0.6 collective-permute-start.11
  163.2 2.1 fusion.17
  165.3 3.4 %collective-permute-done.11 = f32[152,160]{1,0:T(8,128)S(1)} collective-permute-done((f32[152,160]{1,0:T(8,128)S(1)}, f32[152,160]{1,0:T(8,128)S(1)}, u32[]{:S(2)}, u32[]{:S(2)}) %collective-permute-start.11) | collective-permute-done | bytes 97312 | tf_op jit(solution)/shard_map/ppermute | solution.py:93
  168.8 23.4 %collective-permute-done.7 = bf16[152,5632]{1,0:T(8,128)(2,1)S(1)} collective-permute-done((bf16[152,5632]{1,0:T(8,128)(2,1)}, bf16[152,5632]{1,0:T(8,128)(2,1)S(1)}, u32[]{:S(2)}, u32[]{:S(2)}) %collective-permute-start.7) | collective-permute-done | bytes 1712160 | tf_op jit(solution)/shard_map/ppermute | solution.py:47
  192.3 2.3 %collective-permute-start.14 = (bf16[152,3072]{1,0:T(8,128)(2,1)S(1)}, bf16[152,3072]{1,0:T(8,128)(2,1)S(1)}, u32[]{:S(2)}, u32[]{:S(2)}) collective-permute-start(bf16[152,3072]{1,0:T(8,128)(2,1)S(1)} %slice.84), channel_id=1, source_target_pairs={{4,8},{8,4},{5,9},{9,5},{6,10},{10,6},{7,11},{11,7},{20,24},{24,20... | collective-permute-start | bytes 2801672 | tf_op jit(solution)/shard_map/ppermute | solution.py:47
  194.6 0.6 fusion.10
  195.3 9.9 %collective-permute-done.8 = bf16[160,10752]{1,0:T(8,128)(2,1)S(1)} collective-permute-done((bf16[160,10752]{1,0:T(8,128)(2,1)S(1)}, bf16[160,10752]{1,0:T(8,128)(2,1)S(1)}, u32[]{:S(2)}, u32[]{:S(2)}) %collective-permute-start.8) | collective-permute-done | bytes 3440672 | tf_op jit(solution)/shard_map/ppermute | solution.py:47
  205.2 1.1 fusion.14
  206.3 1.3 collective-permute-start.9
  208.0 1.6 collective-permute-done.9
  209.6 1.5 collective-permute-start.13
  211.0 0.7 collective-permute-start.12
  211.7 0.7 fusion.4
  212.5 0.7 fusion.2
  213.2 4.8 %collective-permute-done.14 = bf16[152,3072]{1,0:T(8,128)(2,1)S(1)} collective-permute-done((bf16[152,3072]{1,0:T(8,128)(2,1)S(1)}, bf16[152,3072]{1,0:T(8,128)(2,1)S(1)}, u32[]{:S(2)}, u32[]{:S(2)}) %collective-permute-start.14) | collective-permute-done | bytes 933920 | tf_op jit(solution)/shard_map/ppermute | solution.py:47
  218.0 0.5 fusion.31
  218.6 0.5 fusion.30
  219.1 0.9 collective-permute-done.15
  220.0 0.7 collective-permute-start.18
  220.7 0.7 collective-permute-start.17
  221.3 1.3 collective-permute-start.16
  222.7 5.8 %collective-permute-done.16 = f32[152,160]{1,0:T(8,128)S(1)} collective-permute-done((f32[152,160]{1,0:T(8,128)S(1)}, f32[152,160]{1,0:T(8,128)S(1)}, u32[]{:S(2)}, u32[]{:S(2)}) %collective-permute-start.16) | collective-permute-done | bytes 97312 | tf_op jit(solution)/shard_map/ppermute | solution.py:52
  228.5 0.7 add_add_fusion
  (37 shorter events, 1.2 us)
Async XLA Ops:
  0.0 112.4 %collective-permute-start.2 = (bf16[152,16384]{1,0:T(8,128)(2,1)}, bf16[152,16384]{1,0:T(8,128)(2,1)S(1)}, u32[]{:S(2)}, u32[]{:S(2)}) collective-permute-start(bf16[152,16384]{1,0:T(8,128)(2,1)} %param.2), channel_id=1, source_target_pairs={{4,8},{8,4},{5,9},{9,5},{6,10},{10,6},{7,11},{11,7},{20,24},{24,20... | collective-permute-start | bytes 14942216 | tf_op jit(solution)/shard_map/ppermute | solution.py:47
  3.9 4.2 %copy-start = (bf16[160,16384]{1,0:T(8,128)(2,1)S(1)}, bf16[160,16384]{1,0:T(8,128)(2,1)}, u32[]{:S(2)}) copy-start(bf16[160,16384]{1,0:T(8,128)(2,1)} %param.3) | copy-start | bytes 15728644
  3.9 39.0 %collective-permute-start = (bf16[152,5632]{1,0:T(8,128)(2,1)S(1)}, bf16[152,5632]{1,0:T(8,128)(2,1)}, u32[]{:S(2)}, u32[]{:S(2)}) collective-permute-start(bf16[152,5632]{1,0:T(8,128)(2,1)S(1)} %slice.59), channel_id=1, source_target_pairs={{0,4},{4,0},{8,12},{12,8},{1,5},{5,1},{9,13},{13,9},{2,6},{6,2},{1... | collective-permute-start | bytes 5136392 | tf_op jit(solution)/shard_map/ppermute | solution.py:47
  43.0 77.9 %collective-permute-start.1 = (bf16[152,10752]{1,0:T(8,128)(2,1)}, bf16[152,10752]{1,0:T(8,128)(2,1)}, u32[]{:S(2)}, u32[]{:S(2)}) collective-permute-start(bf16[152,10752]{1,0:T(8,128)(2,1)} %slice.58), channel_id=1, source_target_pairs={{0,4},{4,0},{8,12},{12,8},{1,5},{5,1},{9,13},{13,9},{2,6},{6,2},{1... | collective-permute-start | bytes 9805832 | tf_op jit(solution)/shard_map/ppermute | solution.py:47
  43.4 105.8 %collective-permute-start.4 = (bf16[152,5632]{1,0:T(8,128)(2,1)}, bf16[152,5632]{1,0:T(8,128)(2,1)}, u32[]{:S(2)}, u32[]{:S(2)}) collective-permute-start(bf16[152,5632]{1,0:T(8,128)(2,1)} %collective-permute-done), channel_id=1, source_target_pairs={{4,8},{8,4},{5,9},{9,5},{6,10},{10,6},{7,11},{11,7},{20,24},{24,20... | collective-permute-start | bytes 5136392 | tf_op jit(solution)/shard_map/ppermute | solution.py:47
  112.4 2.8 %copy-start.2 = (bf16[152,16384]{1,0:T(8,128)(2,1)}, bf16[152,16384]{1,0:T(8,128)(2,1)S(1)}, u32[]{:S(2)}) copy-start(bf16[152,16384]{1,0:T(8,128)(2,1)S(1)} %collective-permute-done.2) | copy-start | bytes 14942212
  112.5 43.2 %collective-permute-start.6 = (bf16[152,5632]{1,0:T(8,128)(2,1)S(1)}, bf16[152,5632]{1,0:T(8,128)(2,1)}, u32[]{:S(2)}, u32[]{:S(2)}) collective-permute-start(bf16[152,5632]{1,0:T(8,128)(2,1)S(1)} %slice.77), channel_id=1, source_target_pairs={{4,0},{8,12},{5,1},{9,13},{6,2},{10,14},{7,3},{11,15},{20,16},{24,... | collective-permute-start | bytes 5136392 | tf_op jit(solution)/shard_map/ppermute | solution.py:47
  115.2 17.0 %slice-start = ((s8[5242880]{0:T(1024)(128)(4,1)}), s8[1048576]{0:T(1024)(128)(4,1)S(1)}, s32[]{:S(2)}) async-start(s8[5242880]{0:T(1024)(128)(4,1)} %bitcast.20), calls=%async_computation | async-start | bytes 2097152
  115.2 17.0 %slice-start.1 = ((s8[5242880]{0:T(1024)(128)(4,1)}), s8[4194304]{0:T(1024)(128)(4,1)S(1)}, s32[]{:S(2)}) async-start(s8[5242880]{0:T(1024)(128)(4,1)} %bitcast.20), calls=%async_computation.1 | async-start | bytes 8388608
  120.9 8.7 %copy-start.1 = (bf16[160,10752]{1,0:T(8,128)(2,1)S(1)}, bf16[160,10752]{1,0:T(8,128)(2,1)}, u32[]{:S(2)}) copy-start(bf16[160,10752]{1,0:T(8,128)(2,1)} %slice.60) | copy-start | bytes 10321924
  123.8 32.0 %collective-permute-start.5 = (bf16[152,1024]{1,0:T(8,128)(2,1)S(1)}, bf16[152,1024]{1,0:T(8,128)(2,1)S(1)}, u32[]{:S(2)}, u32[]{:S(2)}) collective-permute-start(bf16[152,1024]{1,0:T(8,128)(2,1)S(1)} %slice.76), channel_id=1, source_target_pairs={{4,8},{8,4},{5,9},{9,5},{6,10},{10,6},{7,11},{11,7},{20,24},{24,20... | collective-permute-start | bytes 933896 | tf_op jit(solution)/shard_map/ppermute | solution.py:47
  126.1 85.6 %collective-permute-start.3 = (bf16[152,6656]{1,0:T(8,128)(2,1)S(1)}, bf16[152,6656]{1,0:T(8,128)(2,1)S(1)}, u32[]{:S(2)}, u32[]{:S(2)}) collective-permute-start(bf16[152,6656]{1,0:T(8,128)(2,1)S(1)} %slice.75), channel_id=1, source_target_pairs={{4,8},{8,4},{5,9},{9,5},{6,10},{10,6},{7,11},{11,7},{20,24},{24,20... | collective-permute-start | bytes 6070280 | tf_op jit(solution)/shard_map/ppermute | solution.py:47
  129.6 75.6 %collective-permute-start.8 = (bf16[160,10752]{1,0:T(8,128)(2,1)S(1)}, bf16[160,10752]{1,0:T(8,128)(2,1)S(1)}, u32[]{:S(2)}, u32[]{:S(2)}) collective-permute-start(bf16[160,10752]{1,0:T(8,128)(2,1)S(1)} %copy-done.1), channel_id=1, source_target_pairs={{0,4},{12,8},{1,5},{13,9},{2,6},{14,10},{3,7},{15,11},{16,20},{28,... | collective-permute-start | bytes 10321928 | tf_op jit(solution)/shard_map/ppermute | solution.py:47
  132.2 27.1 %slice-start.2 = ((s8[4980736]{0:T(1024)(128)(4,1)}), s8[4194304]{0:T(1024)(128)(4,1)S(1)}, s32[]{:S(2)}) async-start(s8[4980736]{0:T(1024)(128)(4,1)} %bitcast.22), calls=%async_computation.2 | async-start | bytes 8388608
  135.3 23.9 %slice-start.3 = ((s8[4980736]{0:T(1024)(128)(4,1)}), s8[786432]{0:T(1024)(128)(4,1)S(1)}, s32[]{:S(2)}) async-start(s8[4980736]{0:T(1024)(128)(4,1)} %bitcast.22), calls=%async_computation.3 | async-start | bytes 1572864
  155.8 36.5 %collective-permute-start.7 = (bf16[152,5632]{1,0:T(8,128)(2,1)}, bf16[152,5632]{1,0:T(8,128)(2,1)S(1)}, u32[]{:S(2)}, u32[]{:S(2)}) collective-permute-start(bf16[152,5632]{1,0:T(8,128)(2,1)} %collective-permute-done.4), channel_id=1, source_target_pairs={{4,0},{8,12},{5,1},{9,13},{6,2},{10,14},{7,3},{11,15},{20,16},{24,... | collective-permute-start | bytes 5136392 | tf_op jit(solution)/shard_map/ppermute | solution.py:47
  160.9 1.7 collective-permute-start.10
  162.6 6.1 %collective-permute-start.11 = (f32[152,160]{1,0:T(8,128)S(1)}, f32[152,160]{1,0:T(8,128)S(1)}, u32[]{:S(2)}, u32[]{:S(2)}) collective-permute-start(f32[152,160]{1,0:T(8,128)S(1)} %slice_select_fusion), channel_id=1, source_target_pairs={{0,2},{1,3},{2,0},{3,1},{4,6},{5,7},{6,4},{7,5},{8,10},{9,11},{10,... | collective-permute-start | bytes 291848 | tf_op jit(solution)/shard_map/ppermute | solution.py:93
  192.3 25.7 %collective-permute-start.14 = (bf16[152,3072]{1,0:T(8,128)(2,1)S(1)}, bf16[152,3072]{1,0:T(8,128)(2,1)S(1)}, u32[]{:S(2)}, u32[]{:S(2)}) collective-permute-start(bf16[152,3072]{1,0:T(8,128)(2,1)S(1)} %slice.84), channel_id=1, source_target_pairs={{4,8},{8,4},{5,9},{9,5},{6,10},{10,6},{7,11},{11,7},{20,24},{24,20... | collective-permute-start | bytes 2801672 | tf_op jit(solution)/shard_map/ppermute | solution.py:47
  206.3 3.3 %collective-permute-start.9 = (f32[152,160]{1,0:T(8,128)S(1)}, f32[152,160]{1,0:T(8,128)S(1)}, u32[]{:S(2)}, u32[]{:S(2)}) collective-permute-start(f32[152,160]{1,0:T(8,128)S(1)} %fusion.14), channel_id=1, source_target_pairs={{1,0},{3,2},{5,4},{7,6},{9,8},{11,10},{13,12},{15,14},{17,16},{19,... | collective-permute-start | bytes 291848 | tf_op jit(solution)/shard_map/ppermute | solution.py:98
  209.6 13.1 %collective-permute-start.13 = (f32[152,160]{1,0:T(8,128)S(1)}, f32[152,160]{1,0:T(8,128)S(1)}, u32[]{:S(2)}, u32[]{:S(2)}) collective-permute-start(f32[152,160]{1,0:T(8,128)S(1)} %add.60), channel_id=1, source_target_pairs={{6,2},{10,14},{22,18},{26,30}} | collective-permute-start | bytes 291848 | tf_op jit(solution)/shard_map/ppermute | solution.py:52
  211.0 11.6 %collective-permute-start.12 = (f32[152,160]{1,0:T(8,128)S(1)}, f32[152,160]{1,0:T(8,128)S(1)}, u32[]{:S(2)}, u32[]{:S(2)}) collective-permute-start(f32[152,160]{1,0:T(8,128)S(1)} %add.60), channel_id=1, source_target_pairs={{4,2},{8,14},{20,18},{24,30}} | collective-permute-start | bytes 291848 | tf_op jit(solution)/shard_map/ppermute | solution.py:52
  218.5 1.4 collective-permute-start.15
  220.0 2.7 %collective-permute-start.18 = (f32[152,160]{1,0:T(8,128)S(1)}, f32[152,160]{1,0:T(8,128)S(1)}, u32[]{:S(2)}, u32[]{:S(2)}) collective-permute-start(f32[152,160]{1,0:T(8,128)S(1)} %add_add_fusion.1), channel_id=1, source_target_pairs={{1,3},{15,13},{17,19},{31,29}} | collective-permute-start | bytes 291848 | tf_op jit(solution)/shard_map/ppermute | solution.py:52
  220.7 2.0 collective-permute-start.17
  221.3 7.1 %collective-permute-start.16 = (f32[152,160]{1,0:T(8,128)S(1)}, f32[152,160]{1,0:T(8,128)S(1)}, u32[]{:S(2)}, u32[]{:S(2)}) collective-permute-start(f32[152,160]{1,0:T(8,128)S(1)} %add_add_fusion.1), channel_id=1, source_target_pairs={{4,6},{8,10},{5,3},{11,13},{20,22},{24,26},{21,19},{27,29}} | collective-permute-start | bytes 291848 | tf_op jit(solution)/shard_map/ppermute | solution.py:52

commit v4 on v3

--- a/solution.py
+++ b/solution.py
@@ -57,9 +57,8 @@
 def line(queries, store):
     depth = queries.shape[1]
     cut = depth * 11 // 32 // 128 * 128
-    start = depth // 16 // 128 * 128
     last = depth * 13 // 16 // 128 * 128 - cut
-    first, body, tail = slice(0, start), slice(start, last), slice(last, None)
+    body, tail = slice(0, last), slice(last, None)
     place = lax.axis_index("docs")
     share = lax.axis_index("proj")
     inner = (place == 1) | (place == 2)
@@ -73,11 +72,10 @@
     ends_rest = along(after(queries[:, cut:], ends_near, far_store), ENDS)
     far_near = along(ends_near, MIDDLE)
     relayed = along(middle[:, :cut], OUTWARD)
-    far_first = along(after(ends_rest[:, first], middle), MIDDLE)
     outer_store = along(after(far_store, middle), INWARD)
     far_body = along(after(ends_rest[:, body], middle), MIDDLE)
-    far_relayed = along(after(far_near, relayed, far_first), OUTWARD)
-    far_tail = along(after(ends_rest[:, tail], far_relayed, far_first), MIDDLE)
+    far_relayed = along(after(far_near, relayed), OUTWARD)
+    far_tail = along(after(ends_rest[:, tail], far_relayed), MIDDLE)
 
     own_part = products(queries, store)
     ends_part = products(ends_near, near_store) + products(ends_rest, far_store)
@@ -94,37 +92,35 @@
         jnp.where(low, kept[rows:], kept[:rows]), "proj", CHIPS
     )
 
-    helped = products(middle[:, cut:], outer_store)
-    helped = helped + lax.ppermute(helped, "proj", [(1, 0), (3, 2)])
-    helped_one = across(helped, [(1, 0, 0, 2), (2, 0, 3, 2)])
+    helped = products(middle[:, cut:], outer_store) + products(far_relayed, near_store)
+    helped = helped + across(
+        helped,
+        [(z, p + odd, z, p + 1 - odd) for z, odd in [(0, 0), (1, 1), (2, 1), (3, 0)] for p in (0, 2)],
+    )
+    helped_one = across(helped, [(1, 0, 0, 2), (2, 0, 3, 2), (0, 1, 0, 3), (3, 3, 3, 1)])
     helped_two = across(helped, [(1, 2, 0, 2), (2, 2, 3, 2)])
+    helped_stays = jnp.where(~inner & (share == jnp.where(left, 3, 1)), helped, 0.0)
+    early = early + helped_one + helped_two + helped_stays
 
-    for_inner = products(far_near, near_store) + products(far_first, far_store[:, first])
-    for_outer = products(far_relayed, near_store)
+    far_part = products(far_near, near_store)
     kept_store = jnp.where(even, far_store[:, tail], outer_store[:, tail])
     given_store = jnp.where(even, outer_store[:, tail], far_store[:, tail])
-    far_body, for_inner, for_outer, kept_store, given_store = lax.optimization_barrier(
-        (far_body, for_inner, for_outer, kept_store, given_store, helped)
-    )[:5]
-    for_inner = for_inner + products(far_body, far_store[:, body])
-    for_outer = (
-        for_outer
-        + products(far_first, outer_store[:, first])
-        + products(far_body, outer_store[:, body])
+    far_body, far_part, kept_store, given_store, helped = lax.optimization_barrier(
+        (far_body, far_part, kept_store, given_store, helped)
     )
-    kept = jnp.where(even, for_inner, for_outer)
-    given = jnp.where(even, for_outer, for_inner)
+    far_part = far_part + products(far_body, far_store[:, body])
+    outer_part = products(far_body, outer_store[:, body])
+    kept = jnp.where(even, far_part, outer_part)
+    given = jnp.where(even, outer_part, far_part)
     kept, given, kept_store, given_store, early = lax.optimization_barrier(
         (kept, given, kept_store, given_store, early)
     )
     given = given + products(far_tail, given_store)
     kept = kept + products(far_tail, kept_store)
     kept = kept + lax.ppermute(given, "proj", CORES)
+    two = across(kept, [(1, 3, 0, 3), (2, 1, 3, 1)])
     one = across(kept, [(1, 0, 1, 2), (2, 0, 2, 2), (1, 1, 0, 3), (2, 3, 3, 1)])
-    two = across(kept, [(1, 3, 0, 3), (2, 1, 3, 1)])
-    three = across(kept, [(0, 1, 0, 3), (3, 3, 3, 1)])
-    stays = jnp.where(share == jnp.where(inner, 2, jnp.where(left, 3, 1)), kept, 0.0)
-    return early + helped_one + helped_two + stays + one + two + three
+    return early + jnp.where(inner & (share == 2), kept, 0.0) + one + two
 
 
 def per_device(queries, store):

time: 230 us -> 229 us (level)
    ppermute x10 -> x9, waiting for transfers between devices: 155 us -> 159 us  [along(): return lax.ppermute(value, 'docs', pairs)]
    ppermute x1, waiting for transfers between devices: 3.43 us -> 0.01 us  [line(): lax.ppermute(jnp.where(low, kept[rows:], kept[:rows]), 'proj', CHIPS)]
    ppermute x10 -> x9, starting transfers between devices: 19.9 us -> 21.8 us  [along(): return lax.ppermute(value, 'docs', pairs)]
    dot_general x14 -> x12, matrix products: 21.3 us -> 20.9 us  [products(): lax.dot_general(rows, docs, (((1,), (1,)), ((), ())), preferred_element_t...]
  transfers between devices with their start and end apart: 19 -> 17, of which waited for: 12 -> 10; matrix products, arithmetic and copies ran while one was open for 15% -> 14% of each run, Pallas kernels for 0% -> 0%
where the time goes in v4:
time: 229 us
  waiting for transfers between devices  168 us (73%)
  starting transfers between devices  27.8 us (12%)
  matrix products  20.9 us (9%)
  local copies, waits for them, and re-layouts  10.8 us (5%)
    ppermute x9, waiting for transfers between devices, along(): return lax.ppermute(value, 'docs', pairs)  159 us
    ppermute x9, starting transfers between devices, along(): return lax.ppermute(value, 'docs', pairs)  21.8 us
    dot_general x12, matrix products, products(): lax.dot_general(rows, docs, (((1,), (1,)), ((), ())), preferred_element_t...  20.9 us
    ppermute x5, waiting for transfers between devices, across(): lax.ppermute(value, ('docs', 'proj'), [(a * parts + b, c * parts + d) for...  8.03 us
    ppermute x5, starting transfers between devices, across(): lax.ppermute(value, ('docs', 'proj'), [(a * parts + b, c * parts + d) for...  5.22 us
  transfers between devices with their start and end apart: 17, of which 10 were waited for; matrix products, arithmetic and copies ran while one was open for 14% of the time, Pallas kernels for 0%

profile of v4, /device:TPU:18, one launch (start us, length us, event | category | flops | bytes accessed | tf_op | source)
XLA Modules:
  0.0 228.5 jit_solution(16043340200271619912)
XLA Ops:
  0.0 2.3 %collective-permute-start.2 = (bf16[152,16384]{1,0:T(8,128)(2,1)}, bf16[152,16384]{1,0:T(8,128)(2,1)S(1)}, u32[]{:S(2)}, u32[]{:S(2)}) collective-permute-start(bf16[152,16384]{1,0:T(8,128)(2,1)} %param.2), channel_id=1, source_target_pairs={{4,8},{8,4},{5,9},{9,5},{6,10},{10,6},{7,11},{11,7},{20,24},{24,20... | collective-permute-start | bytes 14942216 | tf_op jit(solution)/shard_map/ppermute | solution.py:47
  2.4 1.6 slice.49
  3.9 0.3 collective-permute-start
  4.2 4.0 %slice.48 = bf16[152,10752]{1,0:T(8,128)(2,1)} slice(bf16[152,16384]{1,0:T(8,128)(2,1)} %param.2), slice={[0:152], [5632:16384]} | slice | bytes 6537216 | tf_op jit(solution)/shard_map/slice | solution.py:72
  8.2 2.0 slice.50
  10.2 32.7 %collective-permute-done = bf16[152,5632]{1,0:T(8,128)(2,1)} collective-permute-done((bf16[152,5632]{1,0:T(8,128)(2,1)S(1)}, bf16[152,5632]{1,0:T(8,128)(2,1)}, u32[]{:S(2)}, u32[]{:S(2)}) %collective-permute-start) | collective-permute-done | bytes 1712160 | tf_op jit(solution)/shard_map/ppermute | solution.py:47
  43.0 0.5 collective-permute-start.1
  43.4 3.3 %collective-permute-start.4 = (bf16[152,5632]{1,0:T(8,128)(2,1)}, bf16[152,5632]{1,0:T(8,128)(2,1)}, u32[]{:S(2)}, u32[]{:S(2)}) collective-permute-start(bf16[152,5632]{1,0:T(8,128)(2,1)} %collective-permute-done), channel_id=1, source_target_pairs={{4,8},{8,4},{5,9},{9,5},{6,10},{10,6},{7,11},{11,7},{20,24},{24,20... | collective-permute-start | bytes 5136392 | tf_op jit(solution)/shard_map/ppermute | solution.py:47
  46.7 65.7 %collective-permute-done.2 = bf16[152,16384]{1,0:T(8,128)(2,1)S(1)} collective-permute-done((bf16[152,16384]{1,0:T(8,128)(2,1)}, bf16[152,16384]{1,0:T(8,128)(2,1)S(1)}, u32[]{:S(2)}, u32[]{:S(2)}) %collective-permute-start.2) | collective-permute-done | bytes 4980768 | tf_op jit(solution)/shard_map/ppermute | solution.py:47
  112.4 0.1 slice.65
  112.5 2.8 %collective-permute-start.6 = (bf16[152,5632]{1,0:T(8,128)(2,1)S(1)}, bf16[152,5632]{1,0:T(8,128)(2,1)}, u32[]{:S(2)}, u32[]{:S(2)}) collective-permute-start(bf16[152,5632]{1,0:T(8,128)(2,1)S(1)} %slice.65), channel_id=1, source_target_pairs={{4,0},{8,12},{5,1},{9,13},{6,2},{10,14},{7,3},{11,15},{20,16},{24,... | collective-permute-start | bytes 5136392 | tf_op jit(solution)/shard_map/ppermute | solution.py:47
  115.3 1.5 collective-permute-start.5
  116.9 5.5 %fusion.25 = f32[152,160]{1,0:T(8,128)S(1)} fusion(bf16[152,16384]{1,0:T(8,128)(2,1)} %param.2, bf16[160,16384]{1,0:T(8,128)(2,1)} %param.3), kind=kOutput, calls=%fused_computation.36 | convolution fusion | flops 796917760 | bytes 10320896 | tf_op jit(solution)/shard_map/dot_general | solution.py:17
  122.4 1.8 slice.62
  124.2 2.4 %collective-permute-start.3 = (bf16[152,7680]{1,0:T(8,128)(2,1)S(1)}, bf16[152,7680]{1,0:T(8,128)(2,1)S(1)}, u32[]{:S(2)}, u32[]{:S(2)}) collective-permute-start(bf16[152,7680]{1,0:T(8,128)(2,1)S(1)} %slice.62), channel_id=1, source_target_pairs={{4,8},{8,4},{5,9},{9,5},{6,10},{10,6},{7,11},{11,7},{20,24},{24,20... | collective-permute-start | bytes 7004168 | tf_op jit(solution)/shard_map/ppermute | solution.py:47
  126.6 3.1 %fusion.23 = f32[152,160]{1,0:T(8,128)S(1)} fusion(bf16[152,10752]{1,0:T(8,128)(2,1)} %collective-permute-done.1, bf16[160,16384]{1,0:T(8,128)(2,1)S(1)} %bitcast.21), kind=kOutput, calls=%fused_computation.34 | convolution fusion | flops 522977280 | bytes 6806528 | tf_op jit(solution)/shard_map/dot_general | solution.py:17
  129.8 2.2 fusion.17
  132.0 17.2 %collective-permute-done.4 = bf16[152,5632]{1,0:T(8,128)(2,1)} collective-permute-done((bf16[152,5632]{1,0:T(8,128)(2,1)}, bf16[152,5632]{1,0:T(8,128)(2,1)}, u32[]{:S(2)}, u32[]{:S(2)}) %collective-permute-start.4) | collective-permute-done | bytes 1712160 | tf_op jit(solution)/shard_map/ppermute | solution.py:47
  149.2 0.2 collective-permute-done.6
  149.5 4.6 %collective-permute-start.7 = (bf16[152,5632]{1,0:T(8,128)(2,1)}, bf16[152,5632]{1,0:T(8,128)(2,1)S(1)}, u32[]{:S(2)}, u32[]{:S(2)}) collective-permute-start(bf16[152,5632]{1,0:T(8,128)(2,1)} %collective-permute-done.4), channel_id=1, source_target_pairs={{4,0},{8,12},{5,1},{9,13},{6,2},{10,14},{7,3},{11,15},{20,16},{24,... | collective-permute-start | bytes 5136392 | tf_op jit(solution)/shard_map/ppermute | solution.py:47
  154.0 2.1 fusion.8
  156.2 1.6 broadcast_select_fusion.3
  157.8 0.1 collective-permute-start.9
  157.9 2.1 fusion.12
  160.0 1.2 slice.69
  161.3 0.6 collective-permute-start.10
  161.9 26.8 %collective-permute-done.7 = bf16[152,5632]{1,0:T(8,128)(2,1)S(1)} collective-permute-done((bf16[152,5632]{1,0:T(8,128)(2,1)}, bf16[152,5632]{1,0:T(8,128)(2,1)S(1)}, u32[]{:S(2)}, u32[]{:S(2)}) %collective-permute-start.7) | collective-permute-done | bytes 1712160 | tf_op jit(solution)/shard_map/ppermute | solution.py:47
  188.7 4.2 %collective-permute-start.13 = (bf16[152,3072]{1,0:T(8,128)(2,1)S(1)}, bf16[152,3072]{1,0:T(8,128)(2,1)S(1)}, u32[]{:S(2)}, u32[]{:S(2)}) collective-permute-start(bf16[152,3072]{1,0:T(8,128)(2,1)S(1)} %slice.69), channel_id=1, source_target_pairs={{4,8},{8,4},{5,9},{9,5},{6,10},{10,6},{7,11},{11,7},{20,24},{24,20... | collective-permute-start | bytes 2801672 | tf_op jit(solution)/shard_map/ppermute | solution.py:47
  192.9 0.6 fusion.10
  193.6 1.1 fusion.20
  194.7 1.3 collective-permute-start.8
  196.0 0.1 broadcast_select_fusion
  196.1 1.8 collective-permute-done.8
  198.0 1.3 collective-permute-start.12
  199.3 0.7 collective-permute-start.11
  200.0 0.8 fusion.4
  200.8 0.8 broadcast_select_fusion.4
  201.6 0.4 collective-permute-done.12
  202.0 0.1 select_add_fusion
  202.1 15.9 %collective-permute-done.13 = bf16[152,3072]{1,0:T(8,128)(2,1)S(1)} collective-permute-done((bf16[152,3072]{1,0:T(8,128)(2,1)S(1)}, bf16[152,3072]{1,0:T(8,128)(2,1)S(1)}, u32[]{:S(2)}, u32[]{:S(2)}) %collective-permute-start.13) | collective-permute-done | bytes 933920 | tf_op jit(solution)/shard_map/ppermute | solution.py:47
  218.0 0.5 fusion.27
  218.5 0.1 collective-permute-start.14
  218.6 0.5 fusion.26
  219.1 0.9 collective-permute-done.14
  220.0 0.7 collective-permute-start.16
  220.7 1.3 collective-permute-start.15
  222.0 5.8 %collective-permute-done.15 = f32[152,160]{1,0:T(8,128)S(1)} collective-permute-done((f32[152,160]{1,0:T(8,128)S(1)}, f32[152,160]{1,0:T(8,128)S(1)}, u32[]{:S(2)}, u32[]{:S(2)}) %collective-permute-start.15) | collective-permute-done | bytes 97312 | tf_op jit(solution)/shard_map/ppermute | solution.py:52
  227.8 0.7 add_add_fusion
  (27 shorter events, 0.2 us)
Async XLA Ops:
  0.0 112.4 %collective-permute-start.2 = (bf16[152,16384]{1,0:T(8,128)(2,1)}, bf16[152,16384]{1,0:T(8,128)(2,1)S(1)}, u32[]{:S(2)}, u32[]{:S(2)}) collective-permute-start(bf16[152,16384]{1,0:T(8,128)(2,1)} %param.2), channel_id=1, source_target_pairs={{4,8},{8,4},{5,9},{9,5},{6,10},{10,6},{7,11},{11,7},{20,24},{24,20... | collective-permute-start | bytes 14942216 | tf_op jit(solution)/shard_map/ppermute | solution.py:47
  3.9 4.3 %copy-start = (bf16[160,16384]{1,0:T(8,128)(2,1)S(1)}, bf16[160,16384]{1,0:T(8,128)(2,1)}, u32[]{:S(2)}) copy-start(bf16[160,16384]{1,0:T(8,128)(2,1)} %param.3) | copy-start | bytes 15728644
  3.9 39.0 %collective-permute-start = (bf16[152,5632]{1,0:T(8,128)(2,1)S(1)}, bf16[152,5632]{1,0:T(8,128)(2,1)}, u32[]{:S(2)}, u32[]{:S(2)}) collective-permute-start(bf16[152,5632]{1,0:T(8,128)(2,1)S(1)} %slice.49), channel_id=1, source_target_pairs={{0,4},{4,0},{8,12},{12,8},{1,5},{5,1},{9,13},{13,9},{2,6},{6,2},{1... | collective-permute-start | bytes 5136392 | tf_op jit(solution)/shard_map/ppermute | solution.py:47
  43.0 79.5 %collective-permute-start.1 = (bf16[152,10752]{1,0:T(8,128)(2,1)}, bf16[152,10752]{1,0:T(8,128)(2,1)}, u32[]{:S(2)}, u32[]{:S(2)}) collective-permute-start(bf16[152,10752]{1,0:T(8,128)(2,1)} %slice.48), channel_id=1, source_target_pairs={{0,4},{4,0},{8,12},{12,8},{1,5},{5,1},{9,13},{13,9},{2,6},{6,2},{1... | collective-permute-start | bytes 9805832 | tf_op jit(solution)/shard_map/ppermute | solution.py:47
  43.4 105.8 %collective-permute-start.4 = (bf16[152,5632]{1,0:T(8,128)(2,1)}, bf16[152,5632]{1,0:T(8,128)(2,1)}, u32[]{:S(2)}, u32[]{:S(2)}) collective-permute-start(bf16[152,5632]{1,0:T(8,128)(2,1)} %collective-permute-done), channel_id=1, source_target_pairs={{4,8},{8,4},{5,9},{9,5},{6,10},{10,6},{7,11},{11,7},{20,24},{24,20... | collective-permute-start | bytes 5136392 | tf_op jit(solution)/shard_map/ppermute | solution.py:47
  112.4 2.9 %copy-start.1 = (bf16[152,16384]{1,0:T(8,128)(2,1)}, bf16[152,16384]{1,0:T(8,128)(2,1)S(1)}, u32[]{:S(2)}) copy-start(bf16[152,16384]{1,0:T(8,128)(2,1)S(1)} %collective-permute-done.2) | copy-start | bytes 14942212
  112.4 14.2 %slice-start = ((s8[5242880]{0:T(1024)(128)(4,1)}), s8[1048576]{0:T(1024)(128)(4,1)S(1)}, s32[]{:S(2)}) async-start(s8[5242880]{0:T(1024)(128)(4,1)} %bitcast.20), calls=%async_computation | async-start | bytes 2097152
  112.5 36.9 %collective-permute-start.6 = (bf16[152,5632]{1,0:T(8,128)(2,1)S(1)}, bf16[152,5632]{1,0:T(8,128)(2,1)}, u32[]{:S(2)}, u32[]{:S(2)}) collective-permute-start(bf16[152,5632]{1,0:T(8,128)(2,1)S(1)} %slice.65), channel_id=1, source_target_pairs={{4,0},{8,12},{5,1},{9,13},{6,2},{10,14},{7,3},{11,15},{20,16},{24,... | collective-permute-start | bytes 5136392 | tf_op jit(solution)/shard_map/ppermute | solution.py:47
  115.3 11.3 %slice-start.1 = ((s8[5242880]{0:T(1024)(128)(4,1)}), s8[4194304]{0:T(1024)(128)(4,1)S(1)}, s32[]{:S(2)}) async-start(s8[5242880]{0:T(1024)(128)(4,1)} %bitcast.20), calls=%async_computation.1 | async-start | bytes 8388608
  115.3 78.3 %collective-permute-start.5 = (bf16[160,10752]{1,0:T(8,128)(2,1)}, bf16[160,10752]{1,0:T(8,128)(2,1)S(1)}, u32[]{:S(2)}, u32[]{:S(2)}) collective-permute-start(bf16[160,10752]{1,0:T(8,128)(2,1)} %slice.50), channel_id=1, source_target_pairs={{0,4},{12,8},{1,5},{13,9},{2,6},{14,10},{3,7},{15,11},{16,20},{28,... | collective-permute-start | bytes 10321928 | tf_op jit(solution)/shard_map/ppermute | solution.py:47
  124.2 75.7 %collective-permute-start.3 = (bf16[152,7680]{1,0:T(8,128)(2,1)S(1)}, bf16[152,7680]{1,0:T(8,128)(2,1)S(1)}, u32[]{:S(2)}, u32[]{:S(2)}) collective-permute-start(bf16[152,7680]{1,0:T(8,128)(2,1)S(1)} %slice.62), channel_id=1, source_target_pairs={{4,8},{8,4},{5,9},{9,5},{6,10},{10,6},{7,11},{11,7},{20,24},{24,20... | collective-permute-start | bytes 7004168 | tf_op jit(solution)/shard_map/ppermute | solution.py:47
  126.6 29.5 %slice-start.2 = ((s8[4980736]{0:T(1024)(128)(4,1)}), s8[4194304]{0:T(1024)(128)(4,1)S(1)}, s32[]{:S(2)}) async-start(s8[4980736]{0:T(1024)(128)(4,1)} %bitcast.22), calls=%async_computation.2 | async-start | bytes 8388608
  129.8 26.4 %slice-start.3 = ((s8[4980736]{0:T(1024)(128)(4,1)}), s8[786432]{0:T(1024)(128)(4,1)S(1)}, s32[]{:S(2)}) async-start(s8[4980736]{0:T(1024)(128)(4,1)} %bitcast.22), calls=%async_computation.3 | async-start | bytes 1572864
  149.5 39.2 %collective-permute-start.7 = (bf16[152,5632]{1,0:T(8,128)(2,1)}, bf16[152,5632]{1,0:T(8,128)(2,1)S(1)}, u32[]{:S(2)}, u32[]{:S(2)}) collective-permute-start(bf16[152,5632]{1,0:T(8,128)(2,1)} %collective-permute-done.4), channel_id=1, source_target_pairs={{4,0},{8,12},{5,1},{9,13},{6,2},{10,14},{7,3},{11,15},{20,16},{24,... | collective-permute-start | bytes 5136392 | tf_op jit(solution)/shard_map/ppermute | solution.py:47
  157.8 3.4 %collective-permute-start.9 = (f32[304,160]{1,0:T(8,128)S(1)}, f32[304,160]{1,0:T(8,128)S(1)}, u32[]{:S(2)}, u32[]{:S(2)}) collective-permute-start(f32[304,160]{1,0:T(8,128)S(1)} %pad_maximum_fusion), channel_id=1, source_target_pairs={{0,1},{1,0},{2,3},{3,2},{4,5},{5,4},{6,7},{7,6},{8,9},{9,8},{10,11... | collective-permute-start | bytes 583688 | tf_op jit(solution)/shard_map/ppermute | solution.py:89
  161.3 40.3 %collective-permute-start.10 = (f32[152,160]{1,0:T(8,128)S(1)}, f32[152,160]{1,0:T(8,128)S(1)}, u32[]{:S(2)}, u32[]{:S(2)}) collective-permute-start(f32[152,160]{1,0:T(8,128)S(1)} %slice_select_fusion), channel_id=1, source_target_pairs={{0,2},{1,3},{2,0},{3,1},{4,6},{5,7},{6,4},{7,5},{8,10},{9,11},{10,... | collective-permute-start | bytes 291848 | tf_op jit(solution)/shard_map/ppermute | solution.py:91
  188.7 29.3 %collective-permute-start.13 = (bf16[152,3072]{1,0:T(8,128)(2,1)S(1)}, bf16[152,3072]{1,0:T(8,128)(2,1)S(1)}, u32[]{:S(2)}, u32[]{:S(2)}) collective-permute-start(bf16[152,3072]{1,0:T(8,128)(2,1)S(1)} %slice.69), channel_id=1, source_target_pairs={{4,8},{8,4},{5,9},{9,5},{6,10},{10,6},{7,11},{11,7},{20,24},{24,20... | collective-permute-start | bytes 2801672 | tf_op jit(solution)/shard_map/ppermute | solution.py:47
  194.7 3.3 %collective-permute-start.8 = (f32[152,160]{1,0:T(8,128)S(1)}, f32[152,160]{1,0:T(8,128)S(1)}, u32[]{:S(2)}, u32[]{:S(2)}) collective-permute-start(f32[152,160]{1,0:T(8,128)S(1)} %fusion.20), channel_id=1, source_target_pairs={{0,1},{2,3},{5,4},{7,6},{9,8},{11,10},{12,13},{14,15},{16,17},{18,... | collective-permute-start | bytes 291848 | tf_op jit(solution)/shard_map/ppermute | solution.py:52
  198.0 4.0 %collective-permute-start.12 = (f32[152,160]{1,0:T(8,128)S(1)}, f32[152,160]{1,0:T(8,128)S(1)}, u32[]{:S(2)}, u32[]{:S(2)}) collective-permute-start(f32[152,160]{1,0:T(8,128)S(1)} %add.54), channel_id=1, source_target_pairs={{6,2},{10,14},{22,18},{26,30}} | collective-permute-start | bytes 291848 | tf_op jit(solution)/shard_map/ppermute | solution.py:52
  199.3 2.7 %collective-permute-start.11 = (f32[152,160]{1,0:T(8,128)S(1)}, f32[152,160]{1,0:T(8,128)S(1)}, u32[]{:S(2)}, u32[]{:S(2)}) collective-permute-start(f32[152,160]{1,0:T(8,128)S(1)} %add.54), channel_id=1, source_target_pairs={{4,2},{8,14},{1,3},{15,13},{20,18},{24,30},{17,19},{31,29}} | collective-permute-start | bytes 291848 | tf_op jit(solution)/shard_map/ppermute | solution.py:52
  218.5 1.4 collective-permute-start.14
  220.0 2.0 collective-permute-start.16
  220.7 7.1 %collective-permute-start.15 = (f32[152,160]{1,0:T(8,128)S(1)}, f32[152,160]{1,0:T(8,128)S(1)}, u32[]{:S(2)}, u32[]{:S(2)}) collective-permute-start(f32[152,160]{1,0:T(8,128)S(1)} %add_add_fusion.1), channel_id=1, source_target_pairs={{4,6},{8,10},{5,3},{11,13},{20,22},{24,26},{21,19},{27,29}} | collective-permute-start | bytes 291848 | tf_op jit(solution)/shard_map/ppermute | solution.py:52

commit v5 on v4

--- a/solution.py
+++ b/solution.py
@@ -57,7 +57,7 @@
 def line(queries, store):
     depth = queries.shape[1]
     cut = depth * 11 // 32 // 128 * 128
-    last = depth * 13 // 16 // 128 * 128 - cut
+    last = depth * 29 // 32 // 128 * 128 - cut
     body, tail = slice(0, last), slice(last, None)
     place = lax.axis_index("docs")
     share = lax.axis_index("proj")
@@ -120,7 +120,7 @@
     kept = kept + lax.ppermute(given, "proj", CORES)
     two = across(kept, [(1, 3, 0, 3), (2, 1, 3, 1)])
     one = across(kept, [(1, 0, 1, 2), (2, 0, 2, 2), (1, 1, 0, 3), (2, 3, 3, 1)])
-    return early + jnp.where(inner & (share == 2), kept, 0.0) + one + two
+    return early + jnp.where(inner & (share == 2), kept, 0.0) + two + one
 
 
 def per_device(queries, store):

time: 229 us -> 228 us (level)
  starting transfers between devices: 27.8 us -> 25.5 us
    ppermute x9, starting transfers between devices: 21.8 us -> 19.5 us  [along(): return lax.ppermute(value, 'docs', pairs)]
  transfers between devices with their start and end apart: 17 -> 17, of which waited for: 10 -> 11; matrix products, arithmetic and copies ran while one was open for 14% -> 14% of each run, Pallas kernels for 0% -> 0%
where the time goes in v5:
time: 228 us
  waiting for transfers between devices  166 us (73%)
  starting transfers between devices  25.5 us (11%)
  matrix products  22.3 us (10%)
  local copies, waits for them, and re-layouts  12.6 us (6%)
    ppermute x9, waiting for transfers between devices, along(): return lax.ppermute(value, 'docs', pairs)  158 us
    dot_general x12, matrix products, products(): lax.dot_general(rows, docs, (((1,), (1,)), ((), ())), preferred_element_t...  22.3 us
    ppermute x9, starting transfers between devices, along(): return lax.ppermute(value, 'docs', pairs)  19.5 us
    ppermute x5, waiting for transfers between devices, across(): lax.ppermute(value, ('docs', 'proj'), [(a * parts + b, c * parts + d) for...  7.04 us
    ppermute x5, starting transfers between devices, across(): lax.ppermute(value, ('docs', 'proj'), [(a * parts + b, c * parts + d) for...  5.3 us
  transfers between devices with their start and end apart: 17, of which 11 were waited for; matrix products, arithmetic and copies ran while one was open for 14% of the time, Pallas kernels for 0%

profile of v5, /device:TPU:18, one launch (start us, length us, event | category | flops | bytes accessed | tf_op | source)
XLA Modules:
  0.0 227.7 jit_solution(1884143773356920463)
XLA Ops:
  0.0 2.3 %collective-permute-start.2 = (bf16[152,16384]{1,0:T(8,128)(2,1)}, bf16[152,16384]{1,0:T(8,128)(2,1)S(1)}, u32[]{:S(2)}, u32[]{:S(2)}) collective-permute-start(bf16[152,16384]{1,0:T(8,128)(2,1)} %param.2), channel_id=1, source_target_pairs={{4,8},{8,4},{5,9},{9,5},{6,10},{10,6},{7,11},{11,7},{20,24},{24,20... | collective-permute-start | bytes 14942216 | tf_op jit(solution)/shard_map/ppermute | solution.py:47
  2.4 1.6 slice.49
  3.9 0.3 collective-permute-start
  4.2 4.0 %slice.48 = bf16[152,10752]{1,0:T(8,128)(2,1)} slice(bf16[152,16384]{1,0:T(8,128)(2,1)} %param.2), slice={[0:152], [5632:16384]} | slice | bytes 6537216 | tf_op jit(solution)/shard_map/slice | solution.py:72
  8.2 0.2 slice.50
  8.5 34.5 %collective-permute-done = bf16[152,5632]{1,0:T(8,128)(2,1)} collective-permute-done((bf16[152,5632]{1,0:T(8,128)(2,1)S(1)}, bf16[152,5632]{1,0:T(8,128)(2,1)}, u32[]{:S(2)}, u32[]{:S(2)}) %collective-permute-start) | collective-permute-done | bytes 1712160 | tf_op jit(solution)/shard_map/ppermute | solution.py:47
  43.0 0.5 collective-permute-start.1
  43.4 3.3 %collective-permute-start.4 = (bf16[152,5632]{1,0:T(8,128)(2,1)}, bf16[152,5632]{1,0:T(8,128)(2,1)}, u32[]{:S(2)}, u32[]{:S(2)}) collective-permute-start(bf16[152,5632]{1,0:T(8,128)(2,1)} %collective-permute-done), channel_id=1, source_target_pairs={{4,8},{8,4},{5,9},{9,5},{6,10},{10,6},{7,11},{11,7},{20,24},{24,20... | collective-permute-start | bytes 5136392 | tf_op jit(solution)/shard_map/ppermute | solution.py:47
  46.7 65.7 %collective-permute-done.2 = bf16[152,16384]{1,0:T(8,128)(2,1)S(1)} collective-permute-done((bf16[152,16384]{1,0:T(8,128)(2,1)}, bf16[152,16384]{1,0:T(8,128)(2,1)S(1)}, u32[]{:S(2)}, u32[]{:S(2)}) %collective-permute-start.2) | collective-permute-done | bytes 4980768 | tf_op jit(solution)/shard_map/ppermute | solution.py:47
  112.4 2.2 copy-done.1
  114.6 1.3 slice.65
  116.0 2.5 %collective-permute-start.6 = (bf16[152,5632]{1,0:T(8,128)(2,1)}, bf16[152,5632]{1,0:T(8,128)(2,1)}, u32[]{:S(2)}, u32[]{:S(2)}) collective-permute-start(bf16[152,5632]{1,0:T(8,128)(2,1)} %slice.65), channel_id=1, source_target_pairs={{4,0},{8,12},{5,1},{9,13},{6,2},{10,14},{7,3},{11,15},{20,16},{24,... | collective-permute-start | bytes 5136392 | tf_op jit(solution)/shard_map/ppermute | solution.py:47
  118.5 1.3 collective-permute-start.5
  119.8 5.5 %fusion.25 = f32[152,160]{1,0:T(8,128)S(1)} fusion(bf16[152,16384]{1,0:T(8,128)(2,1)} %param.2, bf16[160,16384]{1,0:T(8,128)(2,1)} %param.3), kind=kOutput, calls=%fused_computation.36 | convolution fusion | flops 796917760 | bytes 10320896 | tf_op jit(solution)/shard_map/dot_general | solution.py:17
  125.3 2.1 slice.62
  127.5 2.5 %collective-permute-start.3 = (bf16[152,9216]{1,0:T(8,128)(2,1)S(1)}, bf16[152,9216]{1,0:T(8,128)(2,1)S(1)}, u32[]{:S(2)}, u32[]{:S(2)}) collective-permute-start(bf16[152,9216]{1,0:T(8,128)(2,1)S(1)} %slice.62), channel_id=1, source_target_pairs={{4,8},{8,4},{5,9},{9,5},{6,10},{10,6},{7,11},{11,7},{20,24},{24,20... | collective-permute-start | bytes 8405000 | tf_op jit(solution)/shard_map/ppermute | solution.py:47
  130.0 4.2 %fusion.23 = f32[152,160]{1,0:T(8,128)S(1)} fusion(bf16[152,10752]{1,0:T(8,128)(2,1)} %collective-permute-done.1, bf16[160,16384]{1,0:T(8,128)(2,1)} %param.3), kind=kOutput, calls=%fused_computation.34 | convolution fusion | flops 522977280 | bytes 6806528 | tf_op jit(solution)/shard_map/dot_general | solution.py:17
  134.2 2.2 fusion.17
  136.4 12.8 %collective-permute-done.4 = bf16[152,5632]{1,0:T(8,128)(2,1)} collective-permute-done((bf16[152,5632]{1,0:T(8,128)(2,1)}, bf16[152,5632]{1,0:T(8,128)(2,1)}, u32[]{:S(2)}, u32[]{:S(2)}) %collective-permute-start.4) | collective-permute-done | bytes 1712160 | tf_op jit(solution)/shard_map/ppermute | solution.py:47
  149.2 3.3 %collective-permute-done.6 = bf16[152,5632]{1,0:T(8,128)(2,1)} collective-permute-done((bf16[152,5632]{1,0:T(8,128)(2,1)}, bf16[152,5632]{1,0:T(8,128)(2,1)}, u32[]{:S(2)}, u32[]{:S(2)}) %collective-permute-start.6) | collective-permute-done | bytes 1712160 | tf_op jit(solution)/shard_map/ppermute | solution.py:47
  152.5 4.5 %collective-permute-start.7 = (bf16[152,5632]{1,0:T(8,128)(2,1)}, bf16[152,5632]{1,0:T(8,128)(2,1)S(1)}, u32[]{:S(2)}, u32[]{:S(2)}) collective-permute-start(bf16[152,5632]{1,0:T(8,128)(2,1)} %collective-permute-done.4), channel_id=1, source_target_pairs={{4,0},{8,12},{5,1},{9,13},{6,2},{10,14},{7,3},{11,15},{20,16},{24,... | collective-permute-start | bytes 5136392 | tf_op jit(solution)/shard_map/ppermute | solution.py:47
  157.0 2.1 fusion.8
  159.2 1.7 broadcast_select_fusion.3
  161.0 0.1 collective-permute-start.9
  161.0 2.1 fusion.12
  163.2 1.1 slice.69
  164.3 0.6 collective-permute-start.10
  164.9 26.4 %collective-permute-done.7 = bf16[152,5632]{1,0:T(8,128)(2,1)S(1)} collective-permute-done((bf16[152,5632]{1,0:T(8,128)(2,1)}, bf16[152,5632]{1,0:T(8,128)(2,1)S(1)}, u32[]{:S(2)}, u32[]{:S(2)}) %collective-permute-start.7) | collective-permute-done | bytes 1712160 | tf_op jit(solution)/shard_map/ppermute | solution.py:47
  191.3 2.3 %collective-permute-start.13 = (bf16[152,1536]{1,0:T(8,128)(2,1)S(1)}, bf16[152,1536]{1,0:T(8,128)(2,1)S(1)}, u32[]{:S(2)}, u32[]{:S(2)}) collective-permute-start(bf16[152,1536]{1,0:T(8,128)(2,1)S(1)} %slice.69), channel_id=1, source_target_pairs={{4,8},{8,4},{5,9},{9,5},{6,10},{10,6},{7,11},{11,7},{20,24},{24,20... | collective-permute-start | bytes 1400840 | tf_op jit(solution)/shard_map/ppermute | solution.py:47
  193.7 0.7 fusion.10
  194.3 0.3 collective-permute-done.5
  194.6 1.1 fusion.20
  195.7 1.3 collective-permute-start.8
  197.1 1.9 collective-permute-done.8
  199.0 1.4 collective-permute-start.12
  200.4 0.7 collective-permute-start.11
  201.1 8.0 %collective-permute-done.3 = bf16[152,9216]{1,0:T(8,128)(2,1)S(1)} collective-permute-done((bf16[152,9216]{1,0:T(8,128)(2,1)S(1)}, bf16[152,9216]{1,0:T(8,128)(2,1)S(1)}, u32[]{:S(2)}, u32[]{:S(2)}) %collective-permute-start.3) | collective-permute-done | bytes 2801696 | tf_op jit(solution)/shard_map/ppermute | solution.py:47
  209.1 1.1 fusion.4
  210.2 1.0 broadcast_select_fusion.4
  211.3 6.7 %collective-permute-done.13 = bf16[152,1536]{1,0:T(8,128)(2,1)S(1)} collective-permute-done((bf16[152,1536]{1,0:T(8,128)(2,1)S(1)}, bf16[152,1536]{1,0:T(8,128)(2,1)S(1)}, u32[]{:S(2)}, u32[]{:S(2)}) %collective-permute-start.13) | collective-permute-done | bytes 466976 | tf_op jit(solution)/shard_map/ppermute | solution.py:47
  218.0 0.3 fusion.27
  218.3 0.1 collective-permute-start.14
  218.4 0.3 fusion.26
  218.7 1.1 collective-permute-done.14
  219.8 1.3 collective-permute-start.16
  221.1 0.7 collective-permute-start.15
  221.8 5.1 %collective-permute-done.16 = f32[152,160]{1,0:T(8,128)S(1)} collective-permute-done((f32[152,160]{1,0:T(8,128)S(1)}, f32[152,160]{1,0:T(8,128)S(1)}, u32[]{:S(2)}, u32[]{:S(2)}) %collective-permute-start.16) | collective-permute-done | bytes 97312 | tf_op jit(solution)/shard_map/ppermute | solution.py:52
  226.9 0.7 add_add_fusion
  (27 shorter events, 0.4 us)
Async XLA Ops:
  0.0 112.4 %collective-permute-start.2 = (bf16[152,16384]{1,0:T(8,128)(2,1)}, bf16[152,16384]{1,0:T(8,128)(2,1)S(1)}, u32[]{:S(2)}, u32[]{:S(2)}) collective-permute-start(bf16[152,16384]{1,0:T(8,128)(2,1)} %param.2), channel_id=1, source_target_pairs={{4,8},{8,4},{5,9},{9,5},{6,10},{10,6},{7,11},{11,7},{20,24},{24,20... | collective-permute-start | bytes 14942216 | tf_op jit(solution)/shard_map/ppermute | solution.py:47
  3.9 4.3 %copy-start = (bf16[160,16384]{1,0:T(8,128)(2,1)S(1)}, bf16[160,16384]{1,0:T(8,128)(2,1)}, u32[]{:S(2)}) copy-start(bf16[160,16384]{1,0:T(8,128)(2,1)} %param.3) | copy-start | bytes 15728644
  3.9 39.0 %collective-permute-start = (bf16[152,5632]{1,0:T(8,128)(2,1)S(1)}, bf16[152,5632]{1,0:T(8,128)(2,1)}, u32[]{:S(2)}, u32[]{:S(2)}) collective-permute-start(bf16[152,5632]{1,0:T(8,128)(2,1)S(1)} %slice.49), channel_id=1, source_target_pairs={{0,4},{4,0},{8,12},{12,8},{1,5},{5,1},{9,13},{13,9},{2,6},{6,2},{1... | collective-permute-start | bytes 5136392 | tf_op jit(solution)/shard_map/ppermute | solution.py:47
  43.0 82.4 %collective-permute-start.1 = (bf16[152,10752]{1,0:T(8,128)(2,1)}, bf16[152,10752]{1,0:T(8,128)(2,1)}, u32[]{:S(2)}, u32[]{:S(2)}) collective-permute-start(bf16[152,10752]{1,0:T(8,128)(2,1)} %slice.48), channel_id=1, source_target_pairs={{0,4},{4,0},{8,12},{12,8},{1,5},{5,1},{9,13},{13,9},{2,6},{6,2},{1... | collective-permute-start | bytes 9805832 | tf_op jit(solution)/shard_map/ppermute | solution.py:47
  43.4 105.8 %collective-permute-start.4 = (bf16[152,5632]{1,0:T(8,128)(2,1)}, bf16[152,5632]{1,0:T(8,128)(2,1)}, u32[]{:S(2)}, u32[]{:S(2)}) collective-permute-start(bf16[152,5632]{1,0:T(8,128)(2,1)} %collective-permute-done), channel_id=1, source_target_pairs={{4,8},{8,4},{5,9},{9,5},{6,10},{10,6},{7,11},{11,7},{20,24},{24,20... | collective-permute-start | bytes 5136392 | tf_op jit(solution)/shard_map/ppermute | solution.py:47
  112.4 2.2 copy-start.1
  116.0 36.6 %collective-permute-start.6 = (bf16[152,5632]{1,0:T(8,128)(2,1)}, bf16[152,5632]{1,0:T(8,128)(2,1)}, u32[]{:S(2)}, u32[]{:S(2)}) collective-permute-start(bf16[152,5632]{1,0:T(8,128)(2,1)} %slice.65), channel_id=1, source_target_pairs={{4,0},{8,12},{5,1},{9,13},{6,2},{10,14},{7,3},{11,15},{20,16},{24,... | collective-permute-start | bytes 5136392 | tf_op jit(solution)/shard_map/ppermute | solution.py:47
  118.5 76.1 %collective-permute-start.5 = (bf16[160,10752]{1,0:T(8,128)(2,1)S(1)}, bf16[160,10752]{1,0:T(8,128)(2,1)S(1)}, u32[]{:S(2)}, u32[]{:S(2)}) collective-permute-start(bf16[160,10752]{1,0:T(8,128)(2,1)S(1)} %slice.50), channel_id=1, source_target_pairs={{0,4},{12,8},{1,5},{13,9},{2,6},{14,10},{3,7},{15,11},{16,20},{28,... | collective-permute-start | bytes 10321928 | tf_op jit(solution)/shard_map/ppermute | solution.py:47
  125.3 8.8 %slice-start = ((s8[5242880]{0:T(1024)(128)(4,1)}), s8[4194304]{0:T(1024)(128)(4,1)S(1)}, s32[]{:S(2)}) async-start(s8[5242880]{0:T(1024)(128)(4,1)} %bitcast.20), calls=%async_computation | async-start | bytes 8388608
  127.5 6.7 %slice-start.1 = ((s8[5242880]{0:T(1024)(128)(4,1)}), s8[1048576]{0:T(1024)(128)(4,1)S(1)}, s32[]{:S(2)}) async-start(s8[5242880]{0:T(1024)(128)(4,1)} %bitcast.20), calls=%async_computation.1 | async-start | bytes 2097152
  127.5 81.7 %collective-permute-start.3 = (bf16[152,9216]{1,0:T(8,128)(2,1)S(1)}, bf16[152,9216]{1,0:T(8,128)(2,1)S(1)}, u32[]{:S(2)}, u32[]{:S(2)}) collective-permute-start(bf16[152,9216]{1,0:T(8,128)(2,1)S(1)} %slice.62), channel_id=1, source_target_pairs={{4,8},{8,4},{5,9},{9,5},{6,10},{10,6},{7,11},{11,7},{20,24},{24,20... | collective-permute-start | bytes 8405000 | tf_op jit(solution)/shard_map/ppermute | solution.py:47
  130.0 29.2 %slice-start.2 = ((s8[4980736]{0:T(1024)(128)(4,1)}), s8[4194304]{0:T(1024)(128)(4,1)S(1)}, s32[]{:S(2)}) async-start(s8[4980736]{0:T(1024)(128)(4,1)} %bitcast.22), calls=%async_computation.2 | async-start | bytes 8388608
  134.2 25.0 %slice-start.3 = ((s8[4980736]{0:T(1024)(128)(4,1)}), s8[786432]{0:T(1024)(128)(4,1)S(1)}, s32[]{:S(2)}) async-start(s8[4980736]{0:T(1024)(128)(4,1)} %bitcast.22), calls=%async_computation.3 | async-start | bytes 1572864
  152.5 38.8 %collective-permute-start.7 = (bf16[152,5632]{1,0:T(8,128)(2,1)}, bf16[152,5632]{1,0:T(8,128)(2,1)S(1)}, u32[]{:S(2)}, u32[]{:S(2)}) collective-permute-start(bf16[152,5632]{1,0:T(8,128)(2,1)} %collective-permute-done.4), channel_id=1, source_target_pairs={{4,0},{8,12},{5,1},{9,13},{6,2},{10,14},{7,3},{11,15},{20,16},{24,... | collective-permute-start | bytes 5136392 | tf_op jit(solution)/shard_map/ppermute | solution.py:47
  161.0 3.3 %collective-permute-start.9 = (f32[304,160]{1,0:T(8,128)S(1)}, f32[304,160]{1,0:T(8,128)S(1)}, u32[]{:S(2)}, u32[]{:S(2)}) collective-permute-start(f32[304,160]{1,0:T(8,128)S(1)} %pad_maximum_fusion), channel_id=1, source_target_pairs={{0,1},{1,0},{2,3},{3,2},{4,5},{5,4},{6,7},{7,6},{8,9},{9,8},{10,11... | collective-permute-start | bytes 583688 | tf_op jit(solution)/shard_map/ppermute | solution.py:89
  164.3 46.9 %collective-permute-start.10 = (f32[152,160]{1,0:T(8,128)S(1)}, f32[152,160]{1,0:T(8,128)S(1)}, u32[]{:S(2)}, u32[]{:S(2)}) collective-permute-start(f32[152,160]{1,0:T(8,128)S(1)} %slice_select_fusion), channel_id=1, source_target_pairs={{0,2},{1,3},{2,0},{3,1},{4,6},{5,7},{6,4},{7,5},{8,10},{9,11},{10,... | collective-permute-start | bytes 291848 | tf_op jit(solution)/shard_map/ppermute | solution.py:91
  191.3 26.7 %collective-permute-start.13 = (bf16[152,1536]{1,0:T(8,128)(2,1)S(1)}, bf16[152,1536]{1,0:T(8,128)(2,1)S(1)}, u32[]{:S(2)}, u32[]{:S(2)}) collective-permute-start(bf16[152,1536]{1,0:T(8,128)(2,1)S(1)} %slice.69), channel_id=1, source_target_pairs={{4,8},{8,4},{5,9},{9,5},{6,10},{10,6},{7,11},{11,7},{20,24},{24,20... | collective-permute-start | bytes 1400840 | tf_op jit(solution)/shard_map/ppermute | solution.py:47
  195.7 3.3 %collective-permute-start.8 = (f32[152,160]{1,0:T(8,128)S(1)}, f32[152,160]{1,0:T(8,128)S(1)}, u32[]{:S(2)}, u32[]{:S(2)}) collective-permute-start(f32[152,160]{1,0:T(8,128)S(1)} %fusion.20), channel_id=1, source_target_pairs={{0,1},{2,3},{5,4},{7,6},{9,8},{11,10},{12,13},{14,15},{16,17},{18,... | collective-permute-start | bytes 291848 | tf_op jit(solution)/shard_map/ppermute | solution.py:52
  199.0 12.2 %collective-permute-start.12 = (f32[152,160]{1,0:T(8,128)S(1)}, f32[152,160]{1,0:T(8,128)S(1)}, u32[]{:S(2)}, u32[]{:S(2)}) collective-permute-start(f32[152,160]{1,0:T(8,128)S(1)} %add.54), channel_id=1, source_target_pairs={{6,2},{10,14},{22,18},{26,30}} | collective-permute-start | bytes 291848 | tf_op jit(solution)/shard_map/ppermute | solution.py:52
  200.4 10.8 %collective-permute-start.11 = (f32[152,160]{1,0:T(8,128)S(1)}, f32[152,160]{1,0:T(8,128)S(1)}, u32[]{:S(2)}, u32[]{:S(2)}) collective-permute-start(f32[152,160]{1,0:T(8,128)S(1)} %add.54), channel_id=1, source_target_pairs={{4,2},{8,14},{1,3},{15,13},{20,18},{24,30},{17,19},{31,29}} | collective-permute-start | bytes 291848 | tf_op jit(solution)/shard_map/ppermute | solution.py:52
  218.3 1.4 collective-permute-start.14
  219.8 7.1 %collective-permute-start.16 = (f32[152,160]{1,0:T(8,128)S(1)}, f32[152,160]{1,0:T(8,128)S(1)}, u32[]{:S(2)}, u32[]{:S(2)}) collective-permute-start(f32[152,160]{1,0:T(8,128)S(1)} %add_add_fusion.1), channel_id=1, source_target_pairs={{4,6},{8,10},{5,3},{11,13},{20,22},{24,26},{21,19},{27,29}} | collective-permute-start | bytes 291848 | tf_op jit(solution)/shard_map/ppermute | solution.py:52
  221.1 5.8 %collective-permute-start.15 = (f32[152,160]{1,0:T(8,128)S(1)}, f32[152,160]{1,0:T(8,128)S(1)}, u32[]{:S(2)}, u32[]{:S(2)}) collective-permute-start(f32[152,160]{1,0:T(8,128)S(1)} %add_add_fusion.1), channel_id=1, source_target_pairs={{7,3},{9,13},{23,19},{25,29}} | collective-permute-start | bytes 291848 | tf_op jit(solution)/shard_map/ppermute | solution.py:52
